TPU v7x, 32 devices: a whole 2x2x4 slice. The times are simulated.
32 devices in a mesh: seq: 4 (over y, x), head: 8 (over z, core).
Axes of the slice: x: 2, y: 2, z: 4, core: 2. Of those that a mesh axis runs over, the one named last changes fastest.
Arguments:
- layer_input: bfloat16 [4096, 1024], P(('seq', 'head')), may hold values from -6 to 6
- lengths: int32 [5], replicated, may hold values from 128 to 3201, as said below
- gain_a1: bfloat16 [1024], P(('seq', 'head')), may hold values from 0.5 to 1.5
- lin_q: bfloat16 [1024, 256], P(('seq', 'head')), may hold values from -0.1875 to 0.1875
- lin_k: bfloat16 [1024, 256], P(('seq', 'head')), may hold values from -0.1875 to 0.1875
- lin_v: bfloat16 [1024, 1024], P(('seq', 'head')), may hold values from -0.1875 to 0.1875
- lin_out: bfloat16 [1024, 1024], P(('seq', 'head')), may hold values from -3 to 3
- gain_a2: bfloat16 [1024], P(('seq', 'head')), may hold values from 0.5 to 1.5
- mlp_a_gate: bfloat16 [1024, 2752], P(('seq', 'head')), may hold values from -0.1875 to 0.1875
- mlp_a_up: bfloat16 [1024, 2752], P(('seq', 'head')), may hold values from -0.1875 to 0.1875
- mlp_a_down: bfloat16 [2752, 1024], P(None, ('seq', 'head')), may hold values from -0.109375 to 0.109375
- gain_b1: bfloat16 [1024], P(('seq', 'head')), may hold values from 0.5 to 1.5
- win_q: bfloat16 [1024, 1024], P(('seq', 'head')), may hold values from -0.1875 to 0.1875
- win_k: bfloat16 [1024, 1024], P(('seq', 'head')), may hold values from -0.1875 to 0.1875
- win_v: bfloat16 [1024, 1024], P(('seq', 'head')), may hold values from -0.1875 to 0.1875
- win_out: bfloat16 [1024, 1024], P(('seq', 'head')), may hold values from -1.5 to 1.5
- gain_b2: bfloat16 [1024], P(('seq', 'head')), may hold values from 0.5 to 1.5
- mlp_b_gate: bfloat16 [1024, 2752], P(('seq', 'head')), may hold values from -0.1875 to 0.1875
- mlp_b_up: bfloat16 [1024, 2752], P(('seq', 'head')), may hold values from -0.1875 to 0.1875
- mlp_b_down: bfloat16 [2752, 1024], P(None, ('seq', 'head')), may hold values from -0.109375 to 0.109375
- cotangent: bfloat16 [4096, 1024], P(('seq', 'head')), may hold values from -6 to 6
Outputs:
- mixed: bfloat16 [4096, 1024], P(('seq', 'head'))
- grad_input: float32 [4096, 1024], P(('seq', 'head'))
- grad_gain_a1: float32 [1024], P(('seq', 'head'))
- grad_lin_q: float32 [1024, 256], P(('seq', 'head'))
- grad_lin_k: float32 [1024, 256], P(('seq', 'head'))
- grad_lin_v: float32 [1024, 1024], P(('seq', 'head'))
- grad_lin_out: float32 [1024, 1024], P(('seq', 'head'))
- grad_gain_a2: float32 [1024], P(('seq', 'head'))
- grad_mlp_a_gate: float32 [1024, 2752], P(('seq', 'head'))
- grad_mlp_a_up: float32 [1024, 2752], P(('seq', 'head'))
- grad_mlp_a_down: float32 [2752, 1024], P(None, ('seq', 'head'))
- grad_gain_b1: float32 [1024], P(('seq', 'head'))
- grad_win_q: float32 [1024, 1024], P(('seq', 'head'))
- grad_win_k: float32 [1024, 1024], P(('seq', 'head'))
- grad_win_v: float32 [1024, 1024], P(('seq', 'head'))
- grad_win_out: float32 [1024, 1024], P(('seq', 'head'))
- grad_gain_b2: float32 [1024], P(('seq', 'head'))
- grad_mlp_b_gate: float32 [1024, 2752], P(('seq', 'head'))
- grad_mlp_b_up: float32 [1024, 2752], P(('seq', 'head'))
- grad_mlp_b_down: float32 [2752, 1024], P(None, ('seq', 'head'))
Inputs may be any that keep to these rules, and one draw needn't show every extreme that they name: 5 lengths in packing order summing to 4096: one sequence of 3201 tokens, and the others 128, 128, 256 and 383 in some order, some of them before the long one and the rest after it.
All inputs are finite; a program needn't handle non-finite values.
Results may differ from a plain program's by a relative error of at most 0.025.
Values may be sent and summed in bfloat16 or wider, within the bound.
A program may use at most 448 MiB of HBM per device.

v0:
```python
import jax
import jax.numpy as jnp
from jax import lax
from jax.sharding import PartitionSpec as P

D = 1024
HEADS = 16
FEAT = 16
WINDOW = 64


EPSILON = 1e-05
PRECISE = lax.Precision.HIGHEST


def prefix(shard, axis, join, neutral, backward):
    count = lax.axis_size(axis)
    place = lax.axis_index(axis)
    ahead = count - 1 - place if backward else place
    gathered = jax.tree.map(
        lambda a, kind: lax.all_gather(a.astype(kind), axis),
        shard,
        (jnp.bfloat16, jnp.bfloat16, jnp.bfloat16),
    )
    state = jax.tree.map(lambda a, e: jnp.zeros_like(a) + jnp.asarray(e, a.dtype), shard, neutral)

    def one(step, state):
        source = count - 1 - step if backward else step
        return join(
            state,
            jax.tree.map(
                lambda a, own: lax.dynamic_index_in_dim(a, source, 0, False).astype(own.dtype),
                gathered,
                shard,
            ),
        )

    return lax.fori_loop(0, ahead, one, state)


def shifted(block, axis, distance):
    devices = range(lax.axis_size(axis))
    route = [(i - distance, i) for i in devices if i - distance in devices]
    return lax.ppermute(block, axis, route)


def matmul(left, right):
    return jnp.dot(left, right, preferred_element_type=jnp.float32)


def matmul_tn(left, right):
    return lax.dot_general(
        left, right, (((0,), (0,)), ((), ())), preferred_element_type=jnp.float32
    )


def matmul_nt(left, right):
    return lax.dot_general(
        left, right, (((1,), (1,)), ((), ())), preferred_element_type=jnp.float32
    )


def segment_ids(lengths, positions):
    ends = jnp.cumsum(lengths)
    starts = ends - lengths
    counted = jnp.sum((positions[:, None] >= starts[None, :]).astype(jnp.int32), axis=1)
    return counted - 1


def norm_forward(rows_in, gain_vec):
    inv_rms = lax.rsqrt(jnp.mean(rows_in * rows_in, axis=-1, keepdims=True) + EPSILON)
    return ((rows_in * inv_rms * gain_vec.astype(jnp.float32)).astype(jnp.bfloat16), inv_rms)


def norm_backward(rows_in, inv_rms, gain_vec, upstream):
    gained = upstream * gain_vec.astype(jnp.float32)
    inner = jnp.mean(gained * rows_in, axis=-1, keepdims=True)
    grad_rows = inv_rms * gained - rows_in * inv_rms * inv_rms * inv_rms * inner
    grad_gain = jnp.sum(upstream * rows_in * inv_rms, axis=0)
    return (grad_rows, grad_gain)


def mlp_forward(rows_in, gain_vec, w_gate, w_up, w_down):
    normed, inv_rms = norm_forward(rows_in, gain_vec)
    gate_pre = matmul(normed, w_gate)
    up_pre = matmul(normed, w_up)
    hidden = (jax.nn.silu(gate_pre) * up_pre).astype(jnp.bfloat16)
    return (rows_in + matmul(hidden, w_down), (normed, inv_rms, gate_pre, up_pre, hidden))


def mlp_backward(rows_in, gain_vec, w_gate, w_up, w_down, kept, upstream):
    normed, inv_rms, gate_pre, up_pre, hidden = kept
    upstream_low = upstream.astype(jnp.bfloat16)
    grad_down = matmul_tn(hidden, upstream_low)
    grad_hidden = matmul_nt(upstream_low, w_down)
    sigmoid_g = jax.nn.sigmoid(gate_pre)
    grad_gate = (grad_hidden * up_pre * sigmoid_g * (1.0 + gate_pre * (1.0 - sigmoid_g))).astype(
        jnp.bfloat16
    )
    grad_up = (grad_hidden * gate_pre * sigmoid_g).astype(jnp.bfloat16)
    grad_gate_w = matmul_tn(normed, grad_gate)
    grad_up_w = matmul_tn(normed, grad_up)
    grad_normed = matmul_nt(grad_gate, w_gate) + matmul_nt(grad_up, w_up)
    grad_rows, grad_gain = norm_backward(rows_in, inv_rms, gain_vec, grad_normed)
    return (upstream + grad_rows, (grad_gain, grad_gate_w, grad_up_w, grad_down))


def features(vectors):
    count = vectors.shape[-1]
    leading = vectors.shape[:-1]
    linear = vectors * count ** (-0.25)
    square = (vectors[..., :, None] * vectors[..., None, :]).reshape(leading + (count * count,)) * (
        2.0 * count
    ) ** (-0.5)
    return jnp.concatenate([jnp.ones(leading + (1,), jnp.float32), linear, square], axis=-1)


def feature_back(vectors, grads_in):
    count = vectors.shape[-1]
    linear = grads_in[..., 1 : 1 + count] * count ** (-0.25)
    square = grads_in[..., 1 + count :].reshape(grads_in.shape[:-1] + (count, count))
    both = jnp.einsum("...ij,...j->...i", square, vectors, precision=PRECISE) + jnp.einsum(
        "...ji,...j->...i", square, vectors, precision=PRECISE
    )
    return linear + both * (2.0 * count) ** (-0.5)


def carry_state(earlier, later):
    resets = later[2] > 0.5
    return (
        jnp.where(resets, later[0], earlier[0] + later[0]),
        jnp.where(resets, later[1], earlier[1] + later[1]),
        jnp.maximum(earlier[2], later[2]),
    )


def taylor_linear_forward(q_low, k_low, values_in, segment, seg_before):
    stretch, heads, count = q_low.shape
    keys_in = k_low.astype(jnp.float32)
    lin_coef = count ** (-0.5)
    sq_coef = 0.5 / count
    continues = (segment == seg_before).astype(jnp.float32)
    seg_last = segment[-1]
    in_tail = (segment == seg_last).astype(jnp.float32)
    resets = jnp.reshape((seg_last != seg_before).astype(jnp.float32), (1,))
    k_feats = features(keys_in) * in_tail[:, None, None]
    own_state = jnp.einsum("thx,thv->hxv", k_feats, values_in, precision=PRECISE)
    own_sum = jnp.sum(k_feats, axis=0)
    prefix_state, prefix_sum, prefix_flag = prefix(
        (own_state, own_sum, resets),
        "seq",
        carry_state,
        (jnp.zeros_like(own_state), jnp.zeros_like(own_sum), jnp.zeros_like(resets)),
        False,
    )
    block_rows = min(512, stretch)
    key_index = jnp.arange(stretch, dtype=jnp.int32)

    def run_block(block_id):
        first_row = block_id * block_rows
        q_blk_low = lax.dynamic_slice_in_dim(q_low, first_row, block_rows)
        q_blk = q_blk_low.astype(jnp.float32)
        seg_blk = lax.dynamic_slice_in_dim(segment, first_row, block_rows)
        cont_blk = lax.dynamic_slice_in_dim(continues, first_row, block_rows)
        row_pos = first_row + jnp.arange(block_rows, dtype=jnp.int32)
        allowed = (row_pos[:, None] >= key_index[None, :]) & (seg_blk[:, None] == segment[None, :])
        q_dot_k = jnp.einsum("thf,shf->hts", q_blk_low, k_low, preferred_element_type=jnp.float32)
        scores = jnp.where(
            allowed[None], 1.0 + lin_coef * q_dot_k + sq_coef * q_dot_k * q_dot_k, 0.0
        )
        q_feats = features(q_blk)
        numerator = jnp.einsum("hts,shv->thv", scores, values_in, precision=PRECISE) + cont_blk[
            :, None, None
        ] * jnp.einsum("thx,hxv->thv", q_feats, prefix_state, precision=PRECISE)
        denominator = jnp.sum(scores, axis=2).T + cont_blk[:, None] * jnp.einsum(
            "thx,hx->th", q_feats, prefix_sum, precision=PRECISE
        )
        return (numerator / denominator[:, :, None], denominator)

    attended, denominator = lax.map(run_block, jnp.arange(stretch // block_rows, dtype=jnp.int32))
    return (
        attended.reshape(stretch, heads, -1),
        denominator.reshape(stretch, heads),
        prefix_state,
        prefix_sum,
        resets,
    )


def taylor_backward(
    q_low,
    k_low,
    values_in,
    segment,
    seg_before,
    attended,
    denominator,
    prefix_state,
    prefix_sum,
    resets,
    upstream,
):
    stretch, heads, count = q_low.shape
    queries = q_low.astype(jnp.float32)
    keys_in = k_low.astype(jnp.float32)
    lin_coef = count ** (-0.5)
    sq_coef = 0.5 / count
    continues = (segment == seg_before).astype(jnp.float32)
    seg_last = segment[-1]
    in_tail = (segment == seg_last).astype(jnp.float32)
    grad_num = upstream / denominator[:, :, None]
    grad_den = -jnp.sum(upstream * attended, axis=-1) / denominator
    block_rows = min(512, stretch)
    key_index = jnp.arange(stretch, dtype=jnp.int32)

    def run_block(carried, block_id):
        grad_keys, grad_values, grad_state, grad_sum = carried
        first_row = block_id * block_rows
        q_blk_low = lax.dynamic_slice_in_dim(q_low, first_row, block_rows)
        q_blk = lax.dynamic_slice_in_dim(queries, first_row, block_rows)
        seg_blk = lax.dynamic_slice_in_dim(segment, first_row, block_rows)
        cont_blk = lax.dynamic_slice_in_dim(continues, first_row, block_rows)
        num_blk = lax.dynamic_slice_in_dim(grad_num, first_row, block_rows)
        den_blk = lax.dynamic_slice_in_dim(grad_den, first_row, block_rows)
        row_pos = first_row + jnp.arange(block_rows, dtype=jnp.int32)
        allowed = (row_pos[:, None] >= key_index[None, :]) & (seg_blk[:, None] == segment[None, :])
        q_dot_k = jnp.einsum("thf,shf->hts", q_blk_low, k_low, preferred_element_type=jnp.float32)
        scores = jnp.where(
            allowed[None], 1.0 + lin_coef * q_dot_k + sq_coef * q_dot_k * q_dot_k, 0.0
        )
        grad_scores = (
            jnp.einsum("thv,shv->hts", num_blk, values_in, precision=PRECISE)
            + den_blk.T[:, :, None]
        )
        grad_scores = jnp.where(allowed[None], grad_scores, 0.0)
        grad_values = grad_values + jnp.einsum("hts,thv->shv", scores, num_blk, precision=PRECISE)
        grad_dot = grad_scores * (lin_coef + 2.0 * sq_coef * q_dot_k)
        grad_q = jnp.einsum("hts,shf->thf", grad_dot, keys_in, precision=PRECISE)
        grad_keys = grad_keys + jnp.einsum("hts,thf->shf", grad_dot, q_blk, precision=PRECISE)
        q_feats = features(q_blk) * cont_blk[:, None, None]
        grad_feats = (
            jnp.einsum("thv,hxv->thx", num_blk, prefix_state, precision=PRECISE)
            + den_blk[:, :, None] * prefix_sum[None]
        ) * cont_blk[:, None, None]
        grad_q = grad_q + feature_back(q_blk, grad_feats)
        grad_state = grad_state + jnp.einsum("thx,thv->hxv", q_feats, num_blk, precision=PRECISE)
        grad_sum = grad_sum + jnp.einsum("thx,th->hx", q_feats, den_blk, precision=PRECISE)
        return ((grad_keys, grad_values, grad_state, grad_sum), grad_q)

    initial = (
        jnp.zeros_like(keys_in),
        jnp.zeros_like(values_in),
        jnp.zeros_like(prefix_state),
        jnp.zeros_like(prefix_sum),
    )
    (grad_keys, grad_values, grad_state, grad_sum), grad_q = lax.scan(
        run_block, initial, jnp.arange(stretch // block_rows, dtype=jnp.int32)
    )
    later_state, later_sum, later_flag = prefix(
        (grad_state, grad_sum, resets),
        "seq",
        carry_state,
        (jnp.zeros_like(grad_state), jnp.zeros_like(grad_sum), jnp.zeros_like(resets)),
        True,
    )
    k_feats = features(keys_in) * in_tail[:, None, None]
    grad_kfeat = (
        jnp.einsum("thv,hxv->thx", values_in, later_state, precision=PRECISE) + later_sum[None]
    ) * in_tail[:, None, None]
    grad_keys = grad_keys + feature_back(keys_in, grad_kfeat)
    grad_values = grad_values + jnp.einsum("thx,hxv->thv", k_feats, later_state, precision=PRECISE)
    return (
        grad_q.reshape(stretch, -1),
        grad_keys.reshape(stretch, -1),
        grad_values.reshape(stretch, -1),
    )


def window_forward(queries, keys_in, values_in, segment, seg_ext):
    stretch, heads, head_dim = queries.shape
    rim = seg_ext.shape[0] - stretch
    row_width = heads * head_dim
    rims = jnp.concatenate(
        [
            keys_in[stretch - rim :].reshape(rim, row_width),
            values_in[stretch - rim :].reshape(rim, row_width),
        ],
        axis=1,
    )
    received = shifted(rims, "seq", 1)
    keys_ext = jnp.concatenate(
        [received[:, :row_width].reshape(rim, heads, head_dim), keys_in], axis=0
    )
    values_ext = jnp.concatenate(
        [received[:, row_width:].reshape(rim, heads, head_dim), values_in], axis=0
    )
    block_rows = min(512, stretch)
    scaling = head_dim ** (-0.5)
    offsets = (
        jnp.arange(block_rows, dtype=jnp.int32)[:, None]
        - jnp.arange(block_rows + rim, dtype=jnp.int32)[None, :]
        + rim
    )
    in_window = (offsets >= 0) & (offsets < rim + 1)

    def run_block(block_id):
        first_row = block_id * block_rows
        q_blk = lax.dynamic_slice_in_dim(queries, first_row, block_rows)
        k_blk = lax.dynamic_slice_in_dim(keys_ext, first_row, block_rows + rim)
        v_blk = lax.dynamic_slice_in_dim(values_ext, first_row, block_rows + rim)
        seg_q = lax.dynamic_slice_in_dim(segment, first_row, block_rows)
        seg_k = lax.dynamic_slice_in_dim(seg_ext, first_row, block_rows + rim)
        allowed = in_window & (seg_q[:, None] == seg_k[None, :])
        scores = (
            jnp.einsum("thd,shd->hts", q_blk, k_blk, preferred_element_type=jnp.float32) * scaling
        )
        scores = jnp.where(allowed[None], scores, -1e30)
        row_peak = jnp.max(scores, axis=-1, keepdims=True)
        weights = jnp.exp(scores - row_peak)
        row_total = jnp.sum(weights, axis=-1, keepdims=True)
        probs = (weights / row_total).astype(jnp.bfloat16)
        result = jnp.einsum("hts,shd->thd", probs, v_blk, preferred_element_type=jnp.float32)
        return (result, (row_peak + jnp.log(row_total))[:, :, 0])

    attended, log_total = lax.map(run_block, jnp.arange(stretch // block_rows, dtype=jnp.int32))
    return (attended.reshape(stretch, row_width), log_total, keys_ext, values_ext)


def window_backward(queries, keys_ext, values_ext, segment, seg_ext, log_total, upstream):
    stretch, heads, head_dim = queries.shape
    rim = seg_ext.shape[0] - stretch
    row_width = heads * head_dim
    block_rows = min(512, stretch)
    span = block_rows + rim
    scaling = head_dim ** (-0.5)
    offsets = (
        jnp.arange(block_rows, dtype=jnp.int32)[:, None]
        - jnp.arange(span, dtype=jnp.int32)[None, :]
        + rim
    )
    in_window = (offsets >= 0) & (offsets < rim + 1)

    def run_block(carried, block_id):
        grad_keys, grad_values = carried
        first_row = block_id * block_rows
        q_blk = lax.dynamic_slice_in_dim(queries, first_row, block_rows)
        k_blk = lax.dynamic_slice_in_dim(keys_ext, first_row, span)
        v_blk = lax.dynamic_slice_in_dim(values_ext, first_row, span)
        up_blk = lax.dynamic_slice_in_dim(upstream, first_row, block_rows)
        seg_q = lax.dynamic_slice_in_dim(segment, first_row, block_rows)
        seg_k = lax.dynamic_slice_in_dim(seg_ext, first_row, span)
        allowed = in_window & (seg_q[:, None] == seg_k[None, :])
        scores = (
            jnp.einsum("thd,shd->hts", q_blk, k_blk, preferred_element_type=jnp.float32) * scaling
        )
        probs = jnp.where(allowed[None], jnp.exp(scores - log_total[block_id][:, :, None]), 0.0)
        grad_probs = jnp.einsum("thd,shd->hts", up_blk, v_blk, preferred_element_type=jnp.float32)
        row_dot = jnp.sum(probs * grad_probs, axis=-1, keepdims=True)
        grad_scores = (probs * (grad_probs - row_dot)).astype(jnp.bfloat16)
        grad_q = (
            jnp.einsum("hts,shd->thd", grad_scores, k_blk, preferred_element_type=jnp.float32)
            * scaling
        )
        key_part = (
            jnp.einsum("hts,thd->shd", grad_scores, q_blk, preferred_element_type=jnp.float32)
            * scaling
        )
        value_part = jnp.einsum(
            "hts,thd->shd", probs.astype(jnp.bfloat16), up_blk, preferred_element_type=jnp.float32
        )
        grad_keys = lax.dynamic_update_slice_in_dim(
            grad_keys, lax.dynamic_slice_in_dim(grad_keys, first_row, span) + key_part, first_row, 0
        )
        grad_values = lax.dynamic_update_slice_in_dim(
            grad_values,
            lax.dynamic_slice_in_dim(grad_values, first_row, span) + value_part,
            first_row,
            0,
        )
        return ((grad_keys, grad_values), grad_q)

    zeros_ext = jnp.zeros((stretch + rim, heads, head_dim), jnp.float32)
    (grad_keys, grad_values), grad_q = lax.scan(
        run_block, (zeros_ext, zeros_ext), jnp.arange(stretch // block_rows, dtype=jnp.int32)
    )
    rim_terms = jnp.concatenate(
        [grad_keys[:rim].reshape(rim, row_width), grad_values[:rim].reshape(rim, row_width)], axis=1
    )
    returned = shifted(rim_terms.astype(jnp.bfloat16), "seq", -1).astype(rim_terms.dtype)
    grad_keys = (
        grad_keys[rim:].reshape(stretch, row_width).at[stretch - rim :].add(returned[:, :row_width])
    )
    grad_values = (
        grad_values[rim:]
        .reshape(stretch, row_width)
        .at[stretch - rim :]
        .add(returned[:, row_width:])
    )
    return (grad_q.reshape(stretch, row_width), grad_keys, grad_values)


def split_groups(members, groups):
    return jnp.concatenate(
        [member.reshape(member.shape[0], groups, -1) for member in members], axis=-1
    )


def summed_layer(
    grad_gain_in,
    grad_first,
    grad_second,
    grad_third,
    grad_fourth,
    grad_gain_mid,
    grad_gate,
    grad_up,
    grad_down,
):
    return (
        lax.psum_scatter(grad_gain_in, ("seq", "head"), scatter_dimension=0, tiled=True),
        lax.psum_scatter(grad_first, ("seq", "head"), scatter_dimension=0, tiled=True),
        lax.psum_scatter(grad_second, ("seq", "head"), scatter_dimension=0, tiled=True),
        lax.psum_scatter(grad_third, ("seq", "head"), scatter_dimension=0, tiled=True),
        lax.psum_scatter(grad_fourth, ("seq", "head"), scatter_dimension=0, tiled=True),
        lax.psum_scatter(grad_gain_mid, ("seq", "head"), scatter_dimension=0, tiled=True),
        lax.psum_scatter(grad_gate, ("seq", "head"), scatter_dimension=0, tiled=True),
        lax.psum_scatter(grad_up, ("seq", "head"), scatter_dimension=0, tiled=True),
        lax.psum_scatter(grad_down, ("seq", "head"), scatter_dimension=1, tiled=True),
    )


def on_device(
    layer_input,
    lengths,
    gain_a1,
    lin_q,
    lin_k,
    lin_v,
    lin_out,
    gain_a2,
    mlp_a_gate,
    mlp_a_up,
    mlp_a_down,
    gain_b1,
    win_q,
    win_k,
    win_v,
    win_out,
    gain_b2,
    mlp_b_gate,
    mlp_b_up,
    mlp_b_down,
    cotangent,
):
    full = (
        lax.all_gather(gain_a1, ("seq", "head"), axis=0, tiled=True),
        lax.all_gather(lin_q, ("seq", "head"), axis=0, tiled=True),
        lax.all_gather(lin_k, ("seq", "head"), axis=0, tiled=True),
        lax.all_gather(lin_v, ("seq", "head"), axis=0, tiled=True),
        lax.all_gather(lin_out, ("seq", "head"), axis=0, tiled=True),
        lax.all_gather(gain_a2, ("seq", "head"), axis=0, tiled=True),
        lax.all_gather(mlp_a_gate, ("seq", "head"), axis=0, tiled=True),
        lax.all_gather(mlp_a_up, ("seq", "head"), axis=0, tiled=True),
        lax.all_gather(mlp_a_down, ("seq", "head"), axis=1, tiled=True),
        lax.all_gather(gain_b1, ("seq", "head"), axis=0, tiled=True),
        lax.all_gather(win_q, ("seq", "head"), axis=0, tiled=True),
        lax.all_gather(win_k, ("seq", "head"), axis=0, tiled=True),
        lax.all_gather(win_v, ("seq", "head"), axis=0, tiled=True),
        lax.all_gather(win_out, ("seq", "head"), axis=0, tiled=True),
        lax.all_gather(gain_b2, ("seq", "head"), axis=0, tiled=True),
        lax.all_gather(mlp_b_gate, ("seq", "head"), axis=0, tiled=True),
        lax.all_gather(mlp_b_up, ("seq", "head"), axis=0, tiled=True),
        lax.all_gather(mlp_b_down, ("seq", "head"), axis=1, tiled=True),
    )
    (
        gain_a_in,
        w_lin_q,
        w_lin_k,
        w_lin_v,
        w_lin_out,
        gain_a_mid,
        gate_a_w,
        up_a_w,
        down_a_w,
        gain_b_in,
        w_win_q,
        w_win_k,
        w_win_v,
        w_win_out,
        gain_b_mid,
        gate_b_w,
        up_b_w,
        down_b_w,
    ) = full
    tok_rows = layer_input.shape[0]
    groups = lax.axis_size("head")
    stretch = tok_rows * groups
    local_heads = HEADS // groups
    head_dim = D // HEADS
    stretch_first = lax.axis_index("seq") * stretch
    positions = stretch_first + jnp.arange(stretch, dtype=jnp.int32)
    segment = segment_ids(lengths, positions)
    seg_before = segment_ids(lengths, stretch_first - 1 + jnp.zeros((1,), jnp.int32))[0]
    seg_rim = segment_ids(
        lengths, stretch_first - (WINDOW - 1) + jnp.arange(WINDOW - 1, dtype=jnp.int32)
    )
    seg_ext = jnp.concatenate([seg_rim, segment])
    q_width = local_heads * FEAT
    v_width = local_heads * head_dim
    rows_in = layer_input.astype(jnp.float32)
    normed_a, inv_rms_a = norm_forward(rows_in, gain_a_in)
    taylor_q = matmul(normed_a, w_lin_q).astype(jnp.bfloat16)
    taylor_k = matmul(normed_a, w_lin_k).astype(jnp.bfloat16)
    taylor_v = matmul(normed_a, w_lin_v).astype(jnp.bfloat16)
    packed_a = lax.all_to_all(
        split_groups((taylor_q, taylor_k, taylor_v), groups),
        "head",
        split_axis=1,
        concat_axis=0,
        tiled=True,
    )[:, 0]
    heads_q = packed_a[:, :q_width].reshape(stretch, local_heads, FEAT)
    heads_k = packed_a[:, q_width : 2 * q_width].reshape(stretch, local_heads, FEAT)
    heads_v = packed_a[:, 2 * q_width :].reshape(stretch, local_heads, head_dim).astype(jnp.float32)
    (
        linear_attended_rows,
        linear_denominator,
        partial_state_linear,
        partial_sum_linear,
        sequence_resets_linear,
    ) = taylor_linear_forward(heads_q, heads_k, heads_v, segment, seg_before)
    attended_low = linear_attended_rows.reshape(stretch, v_width).astype(jnp.bfloat16)
    out_tok_a = lax.all_to_all(
        attended_low[:, None, :], "head", split_axis=0, concat_axis=1, tiled=True
    ).reshape(tok_rows, D)
    mixed_a = rows_in + matmul(out_tok_a, w_lin_out)
    layer_a, kept_mlp_a = mlp_forward(mixed_a, gain_a_mid, gate_a_w, up_a_w, down_a_w)
    normed_b, inv_rms_b = norm_forward(layer_a, gain_b_in)
    window_q = matmul(normed_b, w_win_q).astype(jnp.bfloat16)
    window_k = matmul(normed_b, w_win_k).astype(jnp.bfloat16)
    window_v = matmul(normed_b, w_win_v).astype(jnp.bfloat16)
    packed_b = lax.all_to_all(
        split_groups((window_q, window_k, window_v), groups),
        "head",
        split_axis=1,
        concat_axis=0,
        tiled=True,
    )[:, 0]
    wheads_q = packed_b[:, :v_width].reshape(stretch, local_heads, head_dim)
    wheads_k = packed_b[:, v_width : 2 * v_width].reshape(stretch, local_heads, head_dim)
    wheads_v = packed_b[:, 2 * v_width :].reshape(stretch, local_heads, head_dim)
    attended_b, log_total, keys_ext, values_ext = window_forward(
        wheads_q, wheads_k, wheads_v, segment, seg_ext
    )
    out_tok_b = lax.all_to_all(
        attended_b.astype(jnp.bfloat16)[:, None, :], "head", split_axis=0, concat_axis=1, tiled=True
    ).reshape(tok_rows, D)
    mixed_b = layer_a + matmul(out_tok_b, w_win_out)
    layer_b, kept_mlp_b = mlp_forward(mixed_b, gain_b_mid, gate_b_w, up_b_w, down_b_w)
    upstream = cotangent.astype(jnp.float32)
    grad_mid_b, mlp_grads_b = mlp_backward(
        mixed_b, gain_b_mid, gate_b_w, up_b_w, down_b_w, kept_mlp_b, upstream
    )
    mix_low_b = grad_mid_b.astype(jnp.bfloat16)
    grad_wout_b = matmul_tn(out_tok_b, mix_low_b)
    grad_att_b = matmul_nt(mix_low_b, w_win_out).astype(jnp.bfloat16)
    grad_heads_b = lax.all_to_all(
        grad_att_b.reshape(tok_rows, groups, -1), "head", split_axis=1, concat_axis=0, tiled=True
    )[:, 0]
    wgrad_q, wgrad_k, wgrad_v = window_backward(
        wheads_q,
        keys_ext,
        values_ext,
        segment,
        seg_ext,
        log_total,
        grad_heads_b.reshape(stretch, local_heads, head_dim),
    )
    packed_gb = jnp.concatenate(
        [wgrad_q.astype(jnp.bfloat16), wgrad_k.astype(jnp.bfloat16), wgrad_v.astype(jnp.bfloat16)],
        axis=-1,
    )
    grads_tok_b = lax.all_to_all(
        packed_gb[:, None, :], "head", split_axis=0, concat_axis=1, tiled=True
    )
    grad_q_b = grads_tok_b[:, :, :v_width].reshape(tok_rows, D)
    grad_k_b = grads_tok_b[:, :, v_width : 2 * v_width].reshape(tok_rows, D)
    grad_v_b = grads_tok_b[:, :, 2 * v_width :].reshape(tok_rows, D)
    grad_normed_b = (
        matmul_nt(grad_q_b, w_win_q) + matmul_nt(grad_k_b, w_win_k) + matmul_nt(grad_v_b, w_win_v)
    )
    grad_rows_b, grad_gain_b = norm_backward(layer_a, inv_rms_b, gain_b_in, grad_normed_b)
    grad_into_b = grad_mid_b + grad_rows_b
    grads_b = (
        grad_gain_b,
        matmul_tn(normed_b, grad_q_b),
        matmul_tn(normed_b, grad_k_b),
        matmul_tn(normed_b, grad_v_b),
        grad_wout_b,
        mlp_grads_b[0],
        mlp_grads_b[1],
        mlp_grads_b[2],
        mlp_grads_b[3],
    )
    grad_mid_a, mlp_grads_a = mlp_backward(
        mixed_a, gain_a_mid, gate_a_w, up_a_w, down_a_w, kept_mlp_a, grad_into_b
    )
    mix_low_a = grad_mid_a.astype(jnp.bfloat16)
    grad_wout_a = matmul_tn(out_tok_a, mix_low_a)
    grad_att_a = matmul_nt(mix_low_a, w_lin_out).astype(jnp.bfloat16)
    grad_heads_a = lax.all_to_all(
        grad_att_a.reshape(tok_rows, groups, -1), "head", split_axis=1, concat_axis=0, tiled=True
    )[:, 0]
    tgrad_q, tgrad_k, taylor_value_gradient = taylor_backward(
        heads_q,
        heads_k,
        heads_v,
        segment,
        seg_before,
        linear_attended_rows,
        linear_denominator,
        partial_state_linear,
        partial_sum_linear,
        sequence_resets_linear,
        grad_heads_a.reshape(stretch, local_heads, head_dim).astype(jnp.float32),
    )
    packed_ga = jnp.concatenate(
        [
            tgrad_q.astype(jnp.bfloat16),
            tgrad_k.astype(jnp.bfloat16),
            taylor_value_gradient.astype(jnp.bfloat16),
        ],
        axis=-1,
    )
    grads_tok_a = lax.all_to_all(
        packed_ga[:, None, :], "head", split_axis=0, concat_axis=1, tiled=True
    )
    grad_q_a = grads_tok_a[:, :, :q_width].reshape(tok_rows, -1)
    grad_k_a = grads_tok_a[:, :, q_width : 2 * q_width].reshape(tok_rows, -1)
    grad_v_a = grads_tok_a[:, :, 2 * q_width :].reshape(tok_rows, D)
    grad_normed_a = (
        matmul_nt(grad_q_a, w_lin_q) + matmul_nt(grad_k_a, w_lin_k) + matmul_nt(grad_v_a, w_lin_v)
    )
    grad_rows_a, grad_gain_a = norm_backward(rows_in, inv_rms_a, gain_a_in, grad_normed_a)
    grad_into_a = grad_mid_a + grad_rows_a
    grads_a = (
        grad_gain_a,
        matmul_tn(normed_a, grad_q_a),
        matmul_tn(normed_a, grad_k_a),
        matmul_tn(normed_a, grad_v_a),
        grad_wout_a,
        mlp_grads_a[0],
        mlp_grads_a[1],
        mlp_grads_a[2],
        mlp_grads_a[3],
    )
    sums_a = summed_layer(*grads_a)
    sums_b = summed_layer(*grads_b)
    return (
        layer_b.astype(jnp.bfloat16),
        grad_into_a,
        sums_a[0],
        sums_a[1],
        sums_a[2],
        sums_a[3],
        sums_a[4],
        sums_a[5],
        sums_a[6],
        sums_a[7],
        sums_a[8],
        sums_b[0],
        sums_b[1],
        sums_b[2],
        sums_b[3],
        sums_b[4],
        sums_b[5],
        sums_b[6],
        sums_b[7],
        sums_b[8],
    )


def solution(mesh):
    placed = (
        P(("seq", "head"), None),
        P(),
        P(("seq", "head")),
        P(("seq", "head"), None),
        P(("seq", "head"), None),
        P(("seq", "head"), None),
        P(("seq", "head"), None),
        P(("seq", "head")),
        P(("seq", "head"), None),
        P(("seq", "head"), None),
        P(None, ("seq", "head")),
        P(("seq", "head")),
        P(("seq", "head"), None),
        P(("seq", "head"), None),
        P(("seq", "head"), None),
        P(("seq", "head"), None),
        P(("seq", "head")),
        P(("seq", "head"), None),
        P(("seq", "head"), None),
        P(None, ("seq", "head")),
        P(("seq", "head"), None),
    )
    return jax.shard_map(
        on_device,
        mesh=mesh,
        in_specs=placed,
        out_specs=(
            P(("seq", "head"), None),
            P(("seq", "head"), None),
            P(("seq", "head")),
            P(("seq", "head"), None),
            P(("seq", "head"), None),
            P(("seq", "head"), None),
            P(("seq", "head"), None),
            P(("seq", "head")),
            P(("seq", "head"), None),
            P(("seq", "head"), None),
            P(None, ("seq", "head")),
            P(("seq", "head")),
            P(("seq", "head"), None),
            P(("seq", "head"), None),
            P(("seq", "head"), None),
            P(("seq", "head"), None),
            P(("seq", "head")),
            P(("seq", "head"), None),
            P(("seq", "head"), None),
            P(None, ("seq", "head")),
        ),
        check_vma=False,
    )
```

profile of v0, /device:TPU:0, one launch (start us, length us, event | category | flops | bytes accessed | tf_op | source)
XLA Modules:
  0.0 3143.8 jit_solution(4211884175404882182)
XLA Ops:
  18.1 42.2 %all-reduce.10 = (bf16[1024]{0:T(1024)(128)(2,1)S(1)}, bf16[1024]{0:T(1024)(128)(2,1)S(1)}, bf16[1024]{0:T(1024)(128)(2,1)S(1)}, bf16[1024]{0:T(1024)(128)(2,1)S(1)}) all-reduce(bf16[1024]{0:T(1024)(128)(2,1)S(1)} %dynamic-update-slice.6, bf16[1024]{0:T(1024)(128)(2,1)S(1)} %dynamic-update-slice.8, ...), channel_id=1, replica_groups=mesh['seq'=4,'head'=8] {'seq','head'}, use_global_device_ids=true, to_apply=%add | all-reduce | flops 4096 | bytes 16384
  61.4 42.9 %all_gather.85 = bf16[1024,256]{1,0:T(8,128)(2,1)S(1)} all-gather(bf16[32,256]{1,0:T(8,128)(2,1)} %param.40), channel_id=1, replica_groups=mesh['seq'=4,'head'=8] {'seq','head'}, dimensions={0}, use_global_device_ids=true | all-gather | bytes 540672 | tf_op jit(solution)/shard_map/all_gather | solution.py:457
  106.5 39.3 %all_gather.86 = bf16[1024,256]{1,0:T(8,128)(2,1)S(1)} all-gather(bf16[32,256]{1,0:T(8,128)(2,1)S(1)} %copy-done.104), channel_id=1, replica_groups=mesh['seq'=4,'head'=8] {'seq','head'}, dimensions={0}, use_global_device_ids=true | all-gather | bytes 540672 | tf_op jit(solution)/shard_map/all_gather | solution.py:458
  196.2 28.3 while.100
  257.1 19.0 all-gather.25.cloned.1.call-done
  282.3 62.9 %all-gather.27.cloned.1.call-done = bf16[2752,1024]{0,1:T(8,128)(2,1)} async-done(((bf16[2752,32]{0,1:T(8,128)(2,1)}), bf16[2752,1024]{0,1:T(8,128)(2,1)}) %all-gather.27.cloned.1.call-update) | async-done | bytes 5636112 | tf_op jit(solution)/shard_map/all_gather | solution.py:464
  350.0 53.5 %all-gather.33.cloned.1.call-done = bf16[1024,1024]{1,0:T(8,128)(2,1)} async-done(((bf16[32,1024]{1,0:T(8,128)(2,1)}), bf16[1024,1024]{1,0:T(8,128)(2,1)}) %all-gather.33.cloned.1.call-update) | async-done | bytes 2097168 | tf_op jit(solution)/shard_map/all_gather | solution.py:468
  405.6 56.3 %all-gather.31.cloned.1.call-done = bf16[1024,1024]{1,0:T(8,128)(2,1)} async-done(((bf16[32,1024]{1,0:T(8,128)(2,1)}), bf16[1024,1024]{1,0:T(8,128)(2,1)}) %all-gather.31.cloned.1.call-update) | async-done | bytes 2097168 | tf_op jit(solution)/shard_map/all_gather | solution.py:467
  464.0 56.2 %all-gather.29.cloned.1.call-done = bf16[1024,1024]{1,0:T(8,128)(2,1)} async-done(((bf16[32,1024]{1,0:T(8,128)(2,1)}), bf16[1024,1024]{1,0:T(8,128)(2,1)}) %all-gather.29.cloned.1.call-update) | async-done | bytes 2097168 | tf_op jit(solution)/shard_map/all_gather | solution.py:466
  527.7 21.5 all-to-all-done.2
  588.2 63.4 %all-gather.37.cloned.1.call-done = bf16[1024,2752]{1,0:T(8,128)(2,1)} async-done(((bf16[32,2752]{1,0:T(8,128)(2,1)}), bf16[1024,2752]{1,0:T(8,128)(2,1)}) %all-gather.37.cloned.1.call-update) | async-done | bytes 5636112 | tf_op jit(solution)/shard_map/all_gather | solution.py:471
  656.6 64.2 %all-gather.39.cloned.1.call-done = bf16[1024,2752]{1,0:T(8,128)(2,1)} async-done(((bf16[32,2752]{1,0:T(8,128)(2,1)}), bf16[1024,2752]{1,0:T(8,128)(2,1)}) %all-gather.39.cloned.1.call-update) | async-done | bytes 5636112 | tf_op jit(solution)/shard_map/all_gather | solution.py:472
  727.0 62.8 %all-gather.41.cloned.1.call-done = bf16[2752,1024]{0,1:T(8,128)(2,1)} async-done(((bf16[2752,32]{0,1:T(8,128)(2,1)}), bf16[2752,1024]{0,1:T(8,128)(2,1)}) %all-gather.41.cloned.1.call-update) | async-done | bytes 5636112 | tf_op jit(solution)/shard_map/all_gather | solution.py:473
  823.0 38.2 %while.102 = (s32[]{:T(128)}, f32[1087,2,64]{0,2,1:T(8,128)}, f32[1087,2,64]{0,2,1:T(8,128)}, bf16[2,512,2,64]{1,3,2,0:T(8,128)(2,1)}, s32[2]{0:T(128)}, /*index...) while((s32[]{:T(128)}, f32[1087,2,64]{0,2,1:T(8,128)}, ...), condition=%wide.region_21.22_spmd.clone.clone, body=%wide.region_19.21_spmd.clone.sunk.clone | while | flops 384477312 | bytes 47473824 | solution.py:383
  872.4 23.4 all_to_all.120
  935.3 59.8 %while.103 = (s32[]{:T(128)}, f32[1024,2,16]{0,2,1:T(8,128)}, f32[1024,2,64]{0,2,1:T(8,128)}, f32[2,273,64]{1,2,0:T(8,128)}, f32[2,273]{1,0:T(2,128)}, /*index=5...) while((s32[]{:T(128)}, f32[1024,2,16]{0,2,1:T(8,128)}, ...), condition=%wide.region_26.27_spmd.clone.clone, body=%wide.region_25.26_spmd.clone.sunk.clone | while | flops 2497227520 | bytes 91060544 | solution.py:256
  1033.1 15.1 all_to_all.121
  1125.1 38.2 %all-reduce.9 = (f32[1024]{0:T(1024)S(1)}, f32[1024]{0:T(1024)S(1)}, f32[1024]{0:T(1024)S(1)}, f32[1024]{0:T(1024)S(1)}) all-reduce(f32[1024]{0:T(1024)S(1)} %get-tuple-element.944, f32[1024]{0:T(1024)S(1)} %copy-done.103, f32[1024]{0:T(1024)S(1)} %copy-done.105, ...), channel_id=6, replica_groups=mesh['seq'=4,'head'=8] {'seq','head'}, use_global_device_ids=true, to_apply=%region_31.32.clone | all-reduce | flops 4096 | bytes 32768
  1166.6 16.7 reduce-scatter.15.cloned.1.call-done
  1183.3 134.0 %reduce-scatter.17.cloned.1.call-done = f32[32,256]{1,0:T(8,128)} async-done(((f32[1024,256]{1,0:T(8,128)}), f32[32,256]{1,0:T(8,128)}) %reduce-scatter.17.cloned.1.call-update) | async-done | bytes 32784 | tf_op jit(solution)/shard_map/reduce_scatter | solution.py:422
  1317.3 141.4 %reduce-scatter.35.cloned.1.call-done = f32[32,1024]{1,0:T(8,128)} async-done(((f32[1024,1024]{1,0:T(8,128)}), f32[32,1024]{1,0:T(8,128)}) %reduce-scatter.35.cloned.1.call-update) | async-done | bytes 131088 | tf_op jit(solution)/shard_map/reduce_scatter | solution.py:424
  1458.7 142.5 %reduce-scatter.29.cloned.1.call-done = f32[32,1024]{1,0:T(8,128)} async-done(((f32[1024,1024]{1,0:T(8,128)}), f32[32,1024]{1,0:T(8,128)}) %reduce-scatter.29.cloned.1.call-update) | async-done | bytes 131088 | tf_op jit(solution)/shard_map/reduce_scatter | solution.py:421
  1601.3 141.9 %reduce-scatter.31.cloned.1.call-done = f32[32,1024]{1,0:T(8,128)} async-done(((f32[1024,1024]{1,0:T(8,128)}), f32[32,1024]{1,0:T(8,128)}) %reduce-scatter.31.cloned.1.call-update) | async-done | bytes 131088 | tf_op jit(solution)/shard_map/reduce_scatter | solution.py:422
  1743.1 142.3 %reduce-scatter.33.cloned.1.call-done = f32[32,1024]{1,0:T(8,128)} async-done(((f32[1024,1024]{1,0:T(8,128)}), f32[32,1024]{1,0:T(8,128)}) %reduce-scatter.33.cloned.1.call-update) | async-done | bytes 131088 | tf_op jit(solution)/shard_map/reduce_scatter | solution.py:423
  1885.4 142.3 %reduce-scatter.21.cloned.1.call-done = f32[32,1024]{1,0:T(8,128)} async-done(((f32[1024,1024]{1,0:T(8,128)}), f32[32,1024]{1,0:T(8,128)}) %reduce-scatter.21.cloned.1.call-update) | async-done | bytes 131088 | tf_op jit(solution)/shard_map/reduce_scatter | solution.py:424
  2027.8 142.2 %reduce-scatter.19.cloned.1.call-done = f32[32,1024]{1,0:T(8,128)} async-done(((f32[1024,1024]{1,0:T(8,128)}), f32[32,1024]{1,0:T(8,128)}) %reduce-scatter.19.cloned.1.call-update) | async-done | bytes 131088 | tf_op jit(solution)/shard_map/reduce_scatter | solution.py:423
  2170.0 160.4 %reduce-scatter.37.cloned.1.call-done = f32[32,2752]{1,0:T(8,128)} async-done(((f32[1024,2752]{1,0:T(8,128)}), f32[32,2752]{1,0:T(8,128)}) %reduce-scatter.37.cloned.1.call-update) | async-done | bytes 352272 | tf_op jit(solution)/shard_map/reduce_scatter | solution.py:426
  2330.3 161.8 %reduce-scatter.39.cloned.1.call-done = f32[32,2752]{1,0:T(8,128)} async-done(((f32[1024,2752]{1,0:T(8,128)}), f32[32,2752]{1,0:T(8,128)}) %reduce-scatter.39.cloned.1.call-update) | async-done | bytes 352272 | tf_op jit(solution)/shard_map/reduce_scatter | solution.py:427
  2492.1 162.1 %reduce-scatter.41.cloned.1.call-done = f32[2752,32]{0,1:T(8,128)} async-done(((f32[2752,1024]{0,1:T(8,128)}), f32[2752,32]{0,1:T(8,128)}) %reduce-scatter.41.cloned.1.call-update) | async-done | bytes 352272 | tf_op jit(solution)/shard_map/reduce_scatter | solution.py:428
  2654.2 161.0 %reduce-scatter.27.cloned.1.call-done = f32[2752,32]{0,1:T(8,128)} async-done(((f32[2752,1024]{0,1:T(8,128)}), f32[2752,32]{0,1:T(8,128)}) %reduce-scatter.27.cloned.1.call-update) | async-done | bytes 352272 | tf_op jit(solution)/shard_map/reduce_scatter | solution.py:428
  2815.2 161.3 %reduce-scatter.23.cloned.1.call-done = f32[32,2752]{1,0:T(8,128)} async-done(((f32[1024,2752]{1,0:T(8,128)}), f32[32,2752]{1,0:T(8,128)}) %reduce-scatter.23.cloned.1.call-update) | async-done | bytes 352272 | tf_op jit(solution)/shard_map/reduce_scatter | solution.py:426
  2976.5 160.6 %reduce-scatter.25.cloned.1.call-done = f32[32,2752]{1,0:T(8,128)} async-done(((f32[1024,2752]{1,0:T(8,128)}), f32[32,2752]{1,0:T(8,128)}) %reduce-scatter.25.cloned.1.call-update) | async-done | bytes 352272 | tf_op jit(solution)/shard_map/reduce_scatter | solution.py:427
  (688 shorter events, 505.5 us)
Async XLA Ops:
  7.2 140.0 %all-gather.19.cloned.1.call-start = ((), (), s32[]{:S(2)}) async-start(), calls=%async_computation.22 | async-start | bytes 2162688 | tf_op jit(solution)/shard_map/all_gather | solution.py:459
  7.9 241.2 %all-gather.21.cloned.1.call-start = ((), (), s32[]{:S(2)}) async-start(), calls=%async_computation.23 | async-start | bytes 2162688 | tf_op jit(solution)/shard_map/all_gather | solution.py:460
  8.7 242.9 %all-gather.23.cloned.1.call-start = ((), (), s32[]{:S(2)}) async-start(), calls=%async_computation.24 | async-start | bytes 5947392 | tf_op jit(solution)/shard_map/all_gather | solution.py:462
  9.4 266.7 %all-gather.25.cloned.1.call-start = ((), (), s32[]{:S(2)}) async-start(), calls=%async_computation.25 | async-start | bytes 5947392 | tf_op jit(solution)/shard_map/all_gather | solution.py:463
  10.0 335.2 %all-gather.27.cloned.1.call-start = ((), (), s32[]{:S(2)}) async-start(), calls=%async_computation.26 | async-start | bytes 5947392 | tf_op jit(solution)/shard_map/all_gather | solution.py:464
  10.6 392.9 %all-gather.33.cloned.1.call-start = ((), (), s32[]{:S(2)}) async-start(), calls=%async_computation.29 | async-start | bytes 2162688 | tf_op jit(solution)/shard_map/all_gather | solution.py:468
  11.2 450.7 %all-gather.31.cloned.1.call-start = ((), (), s32[]{:S(2)}) async-start(), calls=%async_computation.28 | async-start | bytes 2162688 | tf_op jit(solution)/shard_map/all_gather | solution.py:467
  11.9 508.3 %all-gather.29.cloned.1.call-start = ((), (), s32[]{:S(2)}) async-start(), calls=%async_computation.27 | async-start | bytes 2162688 | tf_op jit(solution)/shard_map/all_gather | solution.py:466
  12.7 573.2 %all-gather.35.cloned.1.call-start = ((), (), s32[]{:S(2)}) async-start(), calls=%async_computation.30 | async-start | bytes 2162688 | tf_op jit(solution)/shard_map/all_gather | solution.py:469
  13.4 638.2 %all-gather.37.cloned.1.call-start = ((), (), s32[]{:S(2)}) async-start(), calls=%async_computation.31 | async-start | bytes 5947392 | tf_op jit(solution)/shard_map/all_gather | solution.py:471
  14.0 706.8 %all-gather.39.cloned.1.call-start = ((), (), s32[]{:S(2)}) async-start(), calls=%async_computation.32 | async-start | bytes 5947392 | tf_op jit(solution)/shard_map/all_gather | solution.py:472
  150.3 22.7 all-to-all-start
  229.4 19.3 all-to-all-start.1
  233.3 556.5 %all-gather.41.cloned.1.call-start = ((), (), s32[]{:S(2)}) async-start(), calls=%async_computation.33 | async-start | bytes 5947392 | tf_op jit(solution)/shard_map/all_gather | solution.py:473
  523.3 25.8 all-to-all-start.2
  572.0 13.3 all-to-all-start.3
  806.1 13.7 all-to-all-start.4
  920.2 13.2 all-to-all-start.6
  923.8 259.5 %reduce-scatter.15.cloned.1.call-start = ((), (), s32[]{:S(2)}) async-start(), calls=%async_computation.34 | async-start | bytes 1081344 | tf_op jit(solution)/shard_map/reduce_scatter | solution.py:421
  1051.1 266.2 %reduce-scatter.17.cloned.1.call-start = ((), (), s32[]{:S(2)}) async-start(), calls=%async_computation.35 | async-start | bytes 1081344 | tf_op jit(solution)/shard_map/reduce_scatter | solution.py:422
  1052.6 406.1 %reduce-scatter.35.cloned.1.call-start = ((), (), s32[]{:S(2)}) async-start(), calls=%async_computation.44 | async-start | bytes 4325376 | tf_op jit(solution)/shard_map/reduce_scatter | solution.py:424
  1055.5 545.7 %reduce-scatter.29.cloned.1.call-start = ((), (), s32[]{:S(2)}) async-start(), calls=%async_computation.41 | async-start | bytes 4325376 | tf_op jit(solution)/shard_map/reduce_scatter | solution.py:421
  1059.3 683.9 %reduce-scatter.31.cloned.1.call-start = ((), (), s32[]{:S(2)}) async-start(), calls=%async_computation.42 | async-start | bytes 4325376 | tf_op jit(solution)/shard_map/reduce_scatter | solution.py:422
  1063.0 822.5 %reduce-scatter.33.cloned.1.call-start = ((), (), s32[]{:S(2)}) async-start(), calls=%async_computation.43 | async-start | bytes 4325376 | tf_op jit(solution)/shard_map/reduce_scatter | solution.py:423
  1066.7 961.1 %reduce-scatter.21.cloned.1.call-start = ((), (), s32[]{:S(2)}) async-start(), calls=%async_computation.37 | async-start | bytes 4325376 | tf_op jit(solution)/shard_map/reduce_scatter | solution.py:424
  1070.4 1099.6 %reduce-scatter.19.cloned.1.call-start = ((), (), s32[]{:S(2)}) async-start(), calls=%async_computation.36 | async-start | bytes 4325376 | tf_op jit(solution)/shard_map/reduce_scatter | solution.py:423
  1073.5 1256.8 %reduce-scatter.37.cloned.1.call-start = ((), (), s32[]{:S(2)}) async-start(), calls=%async_computation.45 | async-start | bytes 11894784 | tf_op jit(solution)/shard_map/reduce_scatter | solution.py:426
  1080.6 1411.5 %reduce-scatter.39.cloned.1.call-start = ((), (), s32[]{:S(2)}) async-start(), calls=%async_computation.46 | async-start | bytes 11894784 | tf_op jit(solution)/shard_map/reduce_scatter | solution.py:427
  1087.6 1566.7 %reduce-scatter.41.cloned.1.call-start = ((), (), s32[]{:S(2)}) async-start(), calls=%async_computation.47 | async-start | bytes 11894784 | tf_op jit(solution)/shard_map/reduce_scatter | solution.py:428
  1094.6 1720.6 %reduce-scatter.27.cloned.1.call-start = ((), (), s32[]{:S(2)}) async-start(), calls=%async_computation.40 | async-start | bytes 11894784 | tf_op jit(solution)/shard_map/reduce_scatter | solution.py:428
  1101.9 1874.6 %reduce-scatter.23.cloned.1.call-start = ((), (), s32[]{:S(2)}) async-start(), calls=%async_computation.38 | async-start | bytes 11894784 | tf_op jit(solution)/shard_map/reduce_scatter | solution.py:426
  1109.0 2028.1 %reduce-scatter.25.cloned.1.call-start = ((), (), s32[]{:S(2)}) async-start(), calls=%async_computation.39 | async-start | bytes 11894784 | tf_op jit(solution)/shard_map/reduce_scatter | solution.py:427
  (136 other events, 2435.6 us)
Sparse Core Ops, SparseCore 0:
  11.0 59.4 all-gather.18
  73.5 55.7 all-gather.20
  132.2 73.0 all-gather.22
  208.0 68.0 all-gather.24
  278.9 66.2 all-gather.26
  348.0 55.4 all-gather.32
  406.5 55.3 all-gather.30
  464.8 55.3 all-gather.28
  523.2 58.4 all-gather.34
  584.4 67.1 all-gather.36
  654.5 66.2 all-gather.38
  723.5 66.2 all-gather.40
  1051.2 131.9 reduce-scatter.14
  1186.0 131.2 reduce-scatter.16
  1320.0 138.6 reduce-scatter.34
  1461.4 139.7 reduce-scatter.28
  1603.9 139.1 reduce-scatter.30
  1745.8 139.5 reduce-scatter.32
  1888.3 139.4 reduce-scatter.20
  2030.5 139.4 reduce-scatter.18
  2172.9 157.4 reduce-scatter.36
  2333.2 158.8 reduce-scatter.38
  2495.0 159.1 reduce-scatter.40
  2657.0 158.1 reduce-scatter.26
  2818.1 158.3 reduce-scatter.22
  2979.2 157.8 reduce-scatter.24
where the time goes:
time: 3150 us; the launch traced here: 3140 us
  waiting for transfers between devices  2490 us (79%)
  blocking collectives  246 us (8%)
  matrix products  234 us (7%)
  local copies, waits for them, and re-layouts  80.1 us (3%)
  other arithmetic  41.2 us (1%)
    reduce_scatter x2, waiting for transfers between devices, summed_layer(): lax.psum_scatter(grad_down, ('seq', 'head'), scatter_dimension=1, tiled=T...  323 us
    reduce_scatter x2, waiting for transfers between devices, summed_layer(): lax.psum_scatter(grad_up, ('seq', 'head'), scatter_dimension=0, tiled=True)  322 us
    reduce_scatter x2, waiting for transfers between devices, summed_layer(): lax.psum_scatter(grad_gate, ('seq', 'head'), scatter_dimension=0, tiled=T...  322 us
    reduce_scatter x2, waiting for transfers between devices, summed_layer(): lax.psum_scatter(grad_third, ('seq', 'head'), scatter_dimension=0, tiled=...  285 us
    reduce_scatter x2, waiting for transfers between devices, summed_layer(): lax.psum_scatter(grad_fourth, ('seq', 'head'), scatter_dimension=0, tiled...  284 us
    reduce_scatter x2, waiting for transfers between devices, summed_layer(): lax.psum_scatter(grad_second, ('seq', 'head'), scatter_dimension=0, tiled...  276 us
    reduce_scatter x2, waiting for transfers between devices, summed_layer(): lax.psum_scatter(grad_first, ('seq', 'head'), scatter_dimension=0, tiled=...  159 us
    unnamed x3, blocking collectives  88.7 us
  transfers between devices with their start and end apart: 34, of which 29 were waited for; matrix products, arithmetic and copies ran while one was open for 6% of the time, Pallas kernels for 0%

commit v1 on v0

v1 whole, which is shorter than its diff:
```python
import functools

import jax
import jax.numpy as jnp
import numpy as np
from jax import lax
from jax.experimental import pallas as pl
from jax.experimental.pallas import tpu as pltpu
from jax.sharding import Mesh
from jax.sharding import PartitionSpec as P

D = 1024
HEADS = 16
FEAT = 16
WINDOW = 64
NTP = 8
RIM = 64
SROWS = 160
EPSILON = 1e-05
AXES = ("sh", "sy", "sx", "hh", "hl")
TP = ("sy", "sx", "hl")
GROUP = ("sh", "hh")
MESH_ID = pl.DeviceIdType.MESH
F32 = jnp.float32
BF16 = jnp.bfloat16
VM = pltpu.VMEM
LIMIT = 56 * 1024 * 1024


def vmem_specs(count):
    return [pl.BlockSpec(memory_space=pltpu.VMEM)] * count


def matmul(left, right):
    return jnp.dot(left, right, preferred_element_type=F32)


def matmul_tn(left, right):
    return lax.dot_general(left, right, (((0,), (0,)), ((), ())), preferred_element_type=F32)


def matmul_nt(left, right):
    return lax.dot_general(left, right, (((1,), (1,)), ((), ())), preferred_element_type=F32)


def plane_place():
    sy, sx, c = lax.axis_index("sy"), lax.axis_index("sx"), lax.axis_index("hl")
    me = sy * 2 + sx
    xn = sy * 2 + (1 - sx)
    yn = (1 - sy) * 2 + sx
    dg = 3 - me
    return me, xn, yn, dg, c, {"sx": 1 - sx}, {"sy": 1 - sy}, {"hl": 1 - c}


def remote(src, dst, ssem, rsem, target):
    copy = pltpu.make_async_remote_copy(
        src_ref=src, dst_ref=dst, send_sem=ssem, recv_sem=rsem, device_id=target, device_id_type=MESH_ID
    )
    copy.start()
    return copy


AG_COPIES = 13
RS_COPIES = 10


def drain(stages):
    for _ in stages:
        pass


def gather_rows(full, ssem, rsem):
    me, xn, yn, dg, c, to_x, to_y, to_c = plane_place()

    def send(k, block, half, target):
        view = full.at[block, c, half]
        return remote(view, view, ssem.at[k], rsem.at[k], target)

    cps = {}
    cps[1] = send(1, me, 0, to_x)
    cps[3] = send(3, me, 1, to_y)
    cps[2] = send(2, me, 1, to_x)
    cps[4] = send(4, me, 0, to_y)
    own = full.at[me, c]
    cps[0] = remote(own, own, ssem.at[0], rsem.at[0], to_c)
    yield
    cps[1].wait_recv()
    cps[5] = send(5, xn, 0, to_y)
    cps[6] = send(6, xn, 0, to_c)
    cps[3].wait_recv()
    cps[7] = send(7, yn, 1, to_x)
    cps[8] = send(8, yn, 1, to_c)
    yield
    cps[2].wait_recv()
    cps[9] = send(9, xn, 1, to_c)
    cps[4].wait_recv()
    cps[10] = send(10, yn, 0, to_c)
    cps[5].wait_recv()
    cps[11] = send(11, dg, 0, to_c)
    cps[7].wait_recv()
    cps[12] = send(12, dg, 1, to_c)
    yield
    for k in (0, 6, 8, 9, 10, 11, 12):
        cps[k].wait_recv()
    for k in range(AG_COPIES):
        cps[k].wait_send()


def scatter_rows(part, own, cb, sb, keep, r1, r2, ssem, rsem):
    me, xn, yn, dg, c, to_x, to_y, to_c = plane_place()
    cps = {}
    for k, block in enumerate((dg, xn, yn, me)):
        cps[k] = remote(part.at[block, 1 - c], cb.at[k], ssem.at[k], rsem.at[k], to_c)

    def both(k, block, half):
        return part[block, c, half].astype(F32) + cb[k, half].astype(F32)

    yield
    cps[0].wait_recv()
    sb[0, 0] = both(0, dg, 0).astype(BF16)
    cps[4] = remote(sb.at[0, 0], r1.at[0, 0], ssem.at[4], rsem.at[4], to_x)
    sb[0, 1] = both(0, dg, 1).astype(BF16)
    cps[5] = remote(sb.at[0, 1], r1.at[1, 0], ssem.at[5], rsem.at[5], to_y)
    cps[1].wait_recv()
    sb[1, 0] = both(1, xn, 0).astype(BF16)
    cps[6] = remote(sb.at[1, 0], r1.at[0, 1], ssem.at[6], rsem.at[6], to_x)
    cps[2].wait_recv()
    sb[2, 1] = both(2, yn, 1).astype(BF16)
    cps[7] = remote(sb.at[2, 1], r1.at[1, 1], ssem.at[7], rsem.at[7], to_y)
    keep[0] = both(2, yn, 0)
    keep[1] = both(1, xn, 1)
    cps[3].wait_recv()
    own[0] = both(3, me, 0)
    own[1] = both(3, me, 1)
    yield
    cps[4].wait_recv()
    sb[2, 0] = (keep[0] + r1[0, 0].astype(F32)).astype(BF16)
    cps[8] = remote(sb.at[2, 0], r2.at[0], ssem.at[8], rsem.at[8], to_y)
    cps[5].wait_recv()
    sb[1, 1] = (keep[1] + r1[1, 0].astype(F32)).astype(BF16)
    cps[9] = remote(sb.at[1, 1], r2.at[1], ssem.at[9], rsem.at[9], to_x)
    yield
    cps[6].wait_recv()
    own[0] += r1[0, 1].astype(F32)
    cps[7].wait_recv()
    own[1] += r1[1, 1].astype(F32)
    cps[8].wait_recv()
    own[0] += r2[0].astype(F32)
    cps[9].wait_recv()
    own[1] += r2[1].astype(F32)
    for k in range(RS_COPIES):
        cps[k].wait_send()


def rs_scratch():
    return [
        VM((2, 64, D), F32),
        VM((4, 2, 64, D), BF16),
        VM((3, 2, 64, D), BF16),
        VM((2, 64, D), F32),
        VM((2, 2, 64, D), BF16),
        VM((2, 64, D), BF16),
        pltpu.SemaphoreType.DMA((RS_COPIES,)),
        pltpu.SemaphoreType.DMA((RS_COPIES,)),
    ]


def ag_scratch():
    return [pltpu.SemaphoreType.DMA((AG_COPIES,)), pltpu.SemaphoreType.DMA((AG_COPIES,))]


def cost(micros):
    return pl.CostEstimate(flops=0, bytes_accessed=int(micros * 3.0e6), transcendentals=0)


def group_place():
    return lax.axis_index("sh") * lax.axis_size("hh") + lax.axis_index("hh")


def group_peer(k, count):
    nhh = lax.axis_size("hh")
    other = lax.rem(group_place() + k, count)
    sh, hh = other // nhh, lax.rem(other, nhh)
    return other, sh, hh, {"sh": sh, "hh": hh}


def place_peer(k):
    coords = {}
    for bit, axis in enumerate(("hl", "sx", "sy")):
        here = lax.axis_index(axis)
        coords[axis] = 1 - here if (k >> bit) & 1 else here
    target = {axis: v for bit, (axis, v) in enumerate(coords.items()) if (k >> bit) & 1}
    return coords["sy"] * 2 + coords["sx"], coords["hl"], target


def barrier_of(plane, group, count):
    barrier = pltpu.get_barrier_semaphore()
    seen = 0
    for k in ((1, 2, 4) if plane == 3 else range(1, 8)) if plane else ():
        _, _, target = place_peer(k)
        pl.semaphore_signal(barrier, inc=1, device_id=target, device_id_type=MESH_ID)
        seen += 1
    if group:
        for k in range(1, count):
            target = group_peer(k, count)[3]
            pl.semaphore_signal(barrier, inc=1, device_id=target, device_id_type=MESH_ID)
            seen += 1
    pl.semaphore_wait(barrier, seen)


class Job:
    def __init__(self, kind, src, cols=None):
        self.kind, self.src, self.cols = kind, src, cols

    def out_shape(self):
        nsh, nhh = lax.axis_size("sh"), lax.axis_size("hh")
        shape = list(self.src.shape)
        if self.cols:
            shape[-1] = self.cols[1]
        if self.kind == "zg":
            shape = [nsh * 4, nhh] + shape[1:]
        if self.kind == "zr":
            shape = [nsh * nhh] + shape
        if self.kind == "zs":
            shape = [nsh * nhh, 4] + shape[2:]
        return jax.ShapeDtypeStruct(tuple(shape), self.src.dtype)


def job_start(kind, cols, src, out, ssem, rsem, lsem, count):
    sh, hh, g = lax.axis_index("sh"), lax.axis_index("hh"), group_place()
    cps = []
    local = None
    if kind == "zg":
        view = src.at[:, :, :, pl.ds(cols[0], cols[1])] if cols else src
        dst = out.at[pl.ds(sh * 4, 4), hh]
        for k in range(1, count):
            cps.append(remote(view, dst, ssem.at[k], rsem.at[k], group_peer(k, count)[3]))
        local = (view, dst)
    if kind == "zr":
        for k in range(1, count):
            cps.append(remote(src, out.at[g], ssem.at[k], rsem.at[k], group_peer(k, count)[3]))
        local = (src, out.at[g])
    if kind == "zs":
        part = lambda psh, phh: (
            src.at[pl.ds(psh * 4, 4), phh, :, :, pl.ds(cols[0], cols[1])]
            if cols
            else src.at[pl.ds(psh * 4, 4), phh]
        )
        for k in range(1, count):
            _, psh, phh, target = group_peer(k, count)
            cps.append(remote(part(psh, phh), out.at[g], ssem.at[k], rsem.at[k], target))
        local = (part(sh, hh), out.at[g])
    if kind == "zt":
        for k in range(1, count):
            other, _, _, target = group_peer(k, count)
            cps.append(remote(src.at[other], out.at[g], ssem.at[k], rsem.at[k], target))
        local = (src.at[g], out.at[g])
    if kind == "pa":
        s, c, _ = place_peer(0)
        for k in range(1, 8):
            ps, pc, target = place_peer(k)
            cps.append(remote(src.at[ps, pc], out.at[s, c], ssem.at[k], rsem.at[k], target))
        local = (src.at[s, c], out.at[s, c])
    cp = pltpu.make_async_copy(local[0], local[1], lsem)
    cp.start()
    return cps, cp


def job_wait(started):
    for cps, cp in started:
        for one in cps:
            one.wait()
        cp.wait()


ANY = pl.BlockSpec(memory_space=pl.ANY)
VMEM = pl.BlockSpec(memory_space=pltpu.VMEM)
SMEM = pl.BlockSpec(memory_space=pltpu.SMEM)


def step(body, ins, outs, scratch, jobs, plane, group, name, collective, micros):
    count = lax.axis_size(GROUP)
    n_in, n_out, n_job = len(ins), len(outs), len(jobs)
    kinds = [(job.kind, job.cols) for job in jobs]
    plane = 7 if any(job.kind == "pa" for job in jobs) else plane
    group = group or any(job.kind != "pa" for job in jobs)
    slots = max(count, 8)

    def kernel(*refs):
        in_refs, refs = refs[:n_in], refs[n_in:]
        sources, refs = refs[:n_job], refs[n_job:]
        out_refs, refs = refs[:n_out], refs[n_out:]
        results, refs = refs[:n_job], refs[n_job:]
        sems, own = (refs[-3:], refs[:-3]) if n_job else ((), refs)
        barrier_of(plane, group, count)
        started = []

        def begin():
            for i, (kind, cols) in enumerate(kinds):
                started.append(
                    job_start(
                        kind, cols, sources[i], results[i],
                        sems[0].at[i], sems[1].at[i], sems[2].at[i], count,
                    )
                )

        body(begin, *in_refs, *out_refs, *own)
        if n_job and not started:
            begin()
        job_wait(started)

    extra = [
        pltpu.SemaphoreType.DMA((n_job, slots)),
        pltpu.SemaphoreType.DMA((n_job, slots)),
        pltpu.SemaphoreType.DMA((n_job,)),
    ]
    result = pl.pallas_call(
        kernel,
        out_shape=tuple(o for o, _ in outs) + tuple(job.out_shape() for job in jobs),
        in_specs=[spec for _, spec in ins] + [ANY] * n_job,
        out_specs=tuple(spec for _, spec in outs) + (ANY,) * n_job,
        scratch_shapes=list(scratch) + (extra if n_job else []),
        compiler_params=pltpu.CompilerParams(
            collective_id=collective, has_side_effects=True, vmem_limit_bytes=LIMIT
        ),
        cost_estimate=cost(micros),
        name=name,
    )(*[v for v, _ in ins], *[job.src for job in jobs])
    return result[:n_out], result[n_out:]


FULL = jax.ShapeDtypeStruct((4, 2, 2, 64, D), BF16)
OWN = jax.ShapeDtypeStruct((2, 64, D), F32)


def flat(full):
    return full.reshape(1024, D)


def blocks(rows):
    return rows.reshape(4, 2, 2, 64, D)


def vmem(*values):
    return [(v, VMEM) for v in values]


def normed_half(u, gain):
    inv = lax.rsqrt(jnp.mean(u * u, axis=-1, keepdims=True) + EPSILON)
    return (u * inv * gain).astype(BF16)


def first(x, lin, jobs, collective):
    count = lax.axis_size(GROUP)
    nsh, nhh = lax.axis_size("sh"), lax.axis_size("hh")

    def body(begin, x_ref, lin_ref, full, mid, lin_full, s1, r1, s2, r2, l2):
        me, _, _, _, c, _, _, _ = plane_place()
        moved = job_start("pa", None, lin_ref, mid, s2.at[0], r2.at[0], l2.at[0], count)
        full[me, c] = x_ref[...]
        stages = gather_rows(full, s1, r1)
        next(stages)
        job_wait([moved])
        spread = job_start("zg", None, mid, lin_full, s2.at[1], r2.at[1], l2.at[1], count)
        next(stages)
        drain(stages)
        begin()
        job_wait([spread])

    slots = max(count, 8)
    return step(
        body,
        vmem(x) + [(lin, ANY)],
        [
            (FULL, VMEM),
            (jax.ShapeDtypeStruct(lin.shape, BF16), ANY),
            (jax.ShapeDtypeStruct((nsh * 4, nhh) + lin.shape[1:], BF16), ANY),
        ],
        ag_scratch()
        + [
            pltpu.SemaphoreType.DMA((2, slots)),
            pltpu.SemaphoreType.DMA((2, slots)),
            pltpu.SemaphoreType.DMA((2,)),
        ],
        jobs, 7, True, "first", collective, 25,
    )


def forward_step(part, u, gain, jobs, collective):
    def body(begin, part, u_ref, gain_ref, unew, full, own, cb, sb, keep, r1, r2, ss, rs, ags, agr):
        me, _, _, _, c, _, _, _ = plane_place()
        stages = scatter_rows(part, own, cb, sb, keep, r1, r2, ss, rs)
        next(stages)
        begin()
        drain(stages)
        for half in range(2):
            u = u_ref[half] + own[half]
            unew[half] = u
            full[me, c, half] = normed_half(u, gain_ref[...])
        drain(gather_rows(full, ags, agr))

    return step(
        body, vmem(blocks(part), u, gain), vmem(OWN, FULL), rs_scratch() + ag_scratch(),
        jobs, 3, False, "forward_step", collective, 28,
    )


def norm_back_half(dn, u, gain, upstream):
    inv = lax.rsqrt(jnp.mean(u * u, axis=-1, keepdims=True) + EPSILON)
    gained = dn * gain
    inner = jnp.mean(gained * u, axis=-1, keepdims=True)
    scaled = u * inv
    grad = upstream + inv * gained - scaled * (inv * inv * inner)
    return grad, jnp.sum(dn * scaled, axis=0, keepdims=True)


def backward_step(part, u, gain, upstream, jobs, collective, last=False):
    def body(begin, part, u_ref, gain_ref, up_ref, gnew, ggain, *rest):
        me, _, _, _, c, _, _, _ = plane_place()
        full, rest = (None, rest) if last else (rest[0], rest[1:])
        stages = scatter_rows(part, *rest[:8])
        next(stages)
        begin()
        drain(stages)
        own = rest[0]
        total = None
        for half in range(2):
            grad, gain_part = norm_back_half(
                own[half], u_ref[half].astype(F32), gain_ref[...], up_ref[half].astype(F32)
            )
            gnew[half] = grad
            total = gain_part if total is None else total + gain_part
            if not last:
                full[me, c, half] = grad.astype(BF16)
        ggain[...] = total
        if not last:
            drain(gather_rows(full, rest[8], rest[9]))

    outs = vmem(OWN, jax.ShapeDtypeStruct((1, D), F32)) + ([] if last else vmem(FULL))
    return step(
        body, vmem(blocks(part), u, gain, upstream), outs,
        rs_scratch() + ([] if last else ag_scratch()),
        jobs, 3, False, "last_backward" if last else "backward_step", collective, 16 if last else 28,
    )


def taylor_tables():
    pick = np.zeros((4, 2, 128, 256), np.float32)
    coef = np.zeros((8, 256), np.float32)
    pairs = [(i, j) for i in range(FEAT) for j in range(i, FEAT)]
    one = 4 * FEAT
    for x, (i, j) in enumerate(pairs):
        coef[:, x] = (2.0 * FEAT) ** -0.5 if i == j else FEAT**-0.5
        for t in range(4):
            pick[t, 0, t * FEAT + i, x] = 1.0
            pick[t, 1, t * FEAT + j, x] = 1.0
    for i in range(FEAT):
        x = len(pairs) + i
        coef[:, x] = FEAT**-0.25
        for t in range(4):
            pick[t, 0, t * FEAT + i, x] = 1.0
            pick[t, 1, one, x] = 1.0
    x = len(pairs) + FEAT
    coef[:, x] = 1.0
    pick[:, 0, one, x] = 1.0
    pick[:, 1, one, x] = 1.0
    shift = np.zeros((128, 128), np.float32)
    for i in range(2 * FEAT):
        shift[2 * FEAT + i, i] = 1.0
    return jnp.asarray(pick, BF16), jnp.asarray(coef, F32), jnp.asarray(shift, BF16)


def lanes(rows, width):
    return lax.broadcasted_iota(jnp.int32, (rows, width), 1)


def group_send(count, st, sm, ssem, rsem):
    g = group_place()
    nhh = lax.axis_size("hh")
    cps = []
    for k in range(1, count):
        other = lax.rem(g + k, count)
        target = {"sh": other // nhh, "hh": lax.rem(other, nhh)}
        cps.append(remote(st.at[g], st.at[g], ssem.at[0, k], rsem.at[0, k], target))
        cps.append(remote(sm.at[g], sm.at[g], ssem.at[1, k], rsem.at[1, k], target))
    return cps


def phi_of(x, pick, coef, t):
    left = matmul(x, pick[t, 0])
    right = matmul(x, pick[t, 1])
    return left, right, (left * right * coef).astype(BF16)


def taylor_forward_kernel(
    count, begin, qkv, seg_col, seg_row, last_ref, before_ref, pick, coef_ref, shift, cot_ref, mix,
    o_ref, y_ref, den_ref, pre_ref, psum_ref, cfull,
    st, sm, phis, ssem, rsem, ags, agr,
):
    g = group_place()
    me, _, _, _, c, _, _, _ = plane_place()
    cfull[me, c] = cot_ref[...]
    stages = gather_rows(cfull, ags, agr)
    next(stages)
    coef = coef_ref[0:1, :]
    left_half = lanes(256, 128) < 64

    def states(s, carry):
        rows = pl.ds(s * 256, 256)
        x = jnp.where(lanes(256, 128) == 4 * FEAT, jnp.ones((), BF16), qkv[rows, 0:128])
        v = qkv[rows, 128:256]
        tail = seg_col[rows, :] == last_ref[rows, :]
        v_tail = jnp.where(tail, v, jnp.zeros((), BF16))
        state = jnp.zeros((256, 128), F32)
        for h in range(2):
            _, _, phi_k = phi_of(x, pick, coef, 2 + h)
            side = left_half if h == 0 else jnp.logical_not(left_half)
            state += matmul_tn(phi_k, jnp.where(side, v_tail, jnp.zeros((), BF16)))
            total = jnp.sum(jnp.where(tail, phi_k.astype(F32), 0.0), axis=0, keepdims=True)
            sm[g, s, h : h + 1, :] = total
            _, _, phi_q = phi_of(x, pick, coef, h)
            phis[h, rows, :] = phi_q
        st[g, s] = state[:SROWS].astype(BF16)
        return carry

    sm[g] = jnp.zeros((4, 8, 256), F32)
    lax.fori_loop(0, 4, states, 0)
    cps = group_send(count, st, sm, ssem, rsem)
    begin()
    next(stages)

    def inner(s, carry):
        rows = pl.ds(s * 256, 256)
        x = qkv[rows, 0:128]
        v = qkv[rows, 128:256]
        k = matmul(x, shift[...]).astype(BF16)
        lane = lanes(256, 128)
        order = lax.broadcasted_iota(jnp.int32, (256, 256), 0) >= lanes(256, 256)
        allowed = order & (seg_col[rows, :] == seg_row[s])
        num = jnp.zeros((256, 128), F32)
        dens = []
        for h in range(2):
            q = jnp.where(lane // FEAT == h, x, jnp.zeros((), BF16))
            dot = matmul_nt(q, k)
            score = jnp.where(allowed, 1.0 + dot * FEAT**-0.5 + dot * dot * (0.5 / FEAT), 0.0)
            side = left_half if h == 0 else jnp.logical_not(left_half)
            num += matmul(score.astype(BF16), jnp.where(side, v, jnp.zeros((), BF16)))
            dens.append(jnp.sum(score, axis=1, keepdims=True))
        y_ref[rows, :] = num
        den_ref[rows, :] = jnp.where(left_half, dens[0], dens[1])
        return carry

    lax.fori_loop(0, 4, inner, 0)
    next(stages)
    for cp in cps:
        cp.wait_recv()

    def finish(s, carry):
        rows = pl.ds(s * 256, 256)

        def add(i, acc):
            state, total = acc
            m = mix[s, i]
            return (
                state + m * st[i // 4, lax.rem(i, 4)].astype(F32),
                total + m * sm[i // 4, lax.rem(i, 4)],
            )

        state, total = lax.fori_loop(
            0, 4 * count, add, (jnp.zeros((SROWS, 128), F32), jnp.zeros((8, 256), F32))
        )
        state = state.astype(BF16)
        pre_ref[s] = state
        psum_ref[s] = total
        cont = seg_col[rows, :] == before_ref[rows, :]
        num = jnp.zeros((256, 128), F32)
        dens = []
        for h in range(2):
            phi_q = phis[h, rows, :]
            side = left_half if h == 0 else jnp.logical_not(left_half)
            part = matmul(phi_q[:, :SROWS], state)
            num = jnp.where(side, part, num)
            dens.append(jnp.sum(phi_q.astype(F32) * total[h : h + 1], axis=1, keepdims=True))
        num = jnp.where(cont, num, 0.0) + y_ref[rows, :]
        den = jnp.where(cont, jnp.where(left_half, dens[0], dens[1]), 0.0) + den_ref[rows, :]
        y = num / den
        y_ref[rows, :] = y
        den_ref[rows, :] = den
        o_ref[rows, :] = y.astype(BF16)
        return carry

    lax.fori_loop(0, 4, finish, 0)
    drain(stages)
    for cp in cps:
        cp.wait_send()


def taylor_forward(qkv, seg, tables, cot, jobs, count, collective):
    return step(
        functools.partial(taylor_forward_kernel, count),
        vmem(qkv, seg["col"], seg["row"], seg["last"], seg["before"], *tables, cot)
        + [(seg["mix"], SMEM)],
        vmem(
            jax.ShapeDtypeStruct((1024, 128), BF16),
            jax.ShapeDtypeStruct((1024, 128), F32),
            jax.ShapeDtypeStruct((1024, 128), F32),
            jax.ShapeDtypeStruct((4, SROWS, 128), BF16),
            jax.ShapeDtypeStruct((4, 8, 256), F32),
            FULL,
        ),
        [
            VM((count, 4, SROWS, 128), BF16),
            VM((count, 4, 8, 256), F32),
            VM((2, 1024, 256), BF16),
            pltpu.SemaphoreType.DMA((2, count)),
            pltpu.SemaphoreType.DMA((2, count)),
        ]
        + ag_scratch(),
        jobs, 3, True, "taylor_forward", collective, 28,
    )


def taylor_backward_kernel(
    count, begin, qkv, do_ref, y_ref, den_ref, pre_ref, psum_ref,
    seg_col, seg_row, last_ref, before_ref, pick, coef_ref, shift, mix, out_ref,
    st, sm, acc, dnum_ref, ddens, ssem, rsem,
):
    g = group_place()
    coef = coef_ref[0:1, :]
    left_half = lanes(256, 128) < 64
    zero = jnp.zeros((), BF16)

    def sides(h):
        return left_half if h == 0 else jnp.logical_not(left_half)

    def feature_back(dphi, left, right, t):
        grad = dphi * coef
        return matmul_nt((grad * right).astype(BF16), pick[t, 0]) + matmul_nt(
            (grad * left).astype(BF16), pick[t, 1]
        )

    def states(s, carry):
        rows = pl.ds(s * 256, 256)
        x = jnp.where(lanes(256, 128) == 4 * FEAT, jnp.ones((), BF16), qkv[rows, 0:128])
        do = do_ref[rows, :].astype(F32)
        den = den_ref[rows, :]
        dnum = do / den
        dnum_low = dnum.astype(BF16)
        dnum_ref[rows, :] = dnum_low
        weighted = dnum * y_ref[rows, :]
        cont = seg_col[rows, :] == before_ref[rows, :]
        d_cont = jnp.where(cont, dnum_low, zero)
        pre = pre_ref[s]
        state = jnp.zeros((256, 128), F32)
        grad = jnp.zeros((256, 128), F32)
        for h in range(2):
            dden = -jnp.sum(jnp.where(sides(h), weighted, 0.0), axis=1, keepdims=True)
            ddens[h, rows, :] = jnp.broadcast_to(dden, (256, 128))
            left, right, phi_q = phi_of(x, pick, coef, h)
            d_side = jnp.where(sides(h), d_cont, zero)
            state += matmul_tn(phi_q, d_side)
            dden_cont = jnp.where(cont, dden, 0.0)
            sm[g, s, h : h + 1, :] = jnp.sum(
                phi_q.astype(F32) * dden_cont, axis=0, keepdims=True
            )
            dphi = jnp.concatenate(
                [matmul_nt(d_side, pre), jnp.zeros((256, 256 - SROWS), F32)], axis=1
            ) + dden_cont * psum_ref[s, h : h + 1, :]
            grad += feature_back(dphi, left, right, h)
        st[g, s] = state[:SROWS].astype(BF16)
        acc[0, rows, :] = grad
        return carry

    sm[g] = jnp.zeros((4, 8, 256), F32)
    lax.fori_loop(0, 4, states, 0)
    cps = group_send(count, st, sm, ssem, rsem)
    begin()

    def inner(s, carry):
        rows = pl.ds(s * 256, 256)
        x = qkv[rows, 0:128]
        v = qkv[rows, 128:256]
        dnum = dnum_ref[rows, :]
        k_low = matmul(x, shift[...]).astype(BF16)
        lane = lanes(256, 128)
        order = lax.broadcasted_iota(jnp.int32, (256, 256), 0) >= lanes(256, 256)
        allowed = order & (seg_col[rows, :] == seg_row[s])
        dq = jnp.zeros((256, 128), F32)
        dk = jnp.zeros((256, 128), F32)
        dv = jnp.zeros((256, 128), F32)
        for h in range(2):
            mine = lane // FEAT == h
            q = jnp.where(mine, x, zero)
            dot = matmul_nt(q, k_low)
            score = jnp.where(allowed, 1.0 + dot * FEAT**-0.5 + dot * dot * (0.5 / FEAT), 0.0)
            d_side = jnp.where(sides(h), dnum, zero)
            dscore = matmul_nt(d_side, v) + ddens[h, rows, 0:1]
            e = jnp.where(allowed, dscore * (FEAT**-0.5 + dot * (1.0 / FEAT)), 0.0).astype(BF16)
            dq += matmul(e, jnp.where(mine, k_low, zero))
            dk += matmul_tn(e, q)
            dv += matmul_tn(score.astype(BF16), d_side)
        acc[0, rows, :] += dq
        acc[1, rows, :] = dk
        acc[2, rows, :] = dv
        return carry

    lax.fori_loop(0, 4, inner, 0)
    for cp in cps:
        cp.wait_recv()

    def finish(s, carry):
        rows = pl.ds(s * 256, 256)

        def add(i, both):
            state, total = both
            m = mix[s, i]
            return (
                state + m * st[i // 4, lax.rem(i, 4)].astype(F32),
                total + m * sm[i // 4, lax.rem(i, 4)],
            )

        state, total = lax.fori_loop(
            0, 4 * count, add, (jnp.zeros((SROWS, 128), F32), jnp.zeros((8, 256), F32))
        )
        state = state.astype(BF16)
        x = jnp.where(lanes(256, 128) == 4 * FEAT, jnp.ones((), BF16), qkv[rows, 0:128])
        tail = seg_col[rows, :] == last_ref[rows, :]
        v_tail = jnp.where(tail, qkv[rows, 128:256], zero)
        grad = acc[0, rows, :]
        lane = lanes(256, 128)
        dv = jnp.zeros((256, 128), F32)
        for h in range(2):
            left, right, phi_k = phi_of(x, pick, coef, 2 + h)
            dphi = jnp.concatenate(
                [
                    matmul_nt(jnp.where(sides(h), v_tail, zero), state),
                    jnp.zeros((256, 256 - SROWS), F32),
                ],
                axis=1,
            ) + jnp.where(tail, total[h : h + 1], 0.0)
            grad += feature_back(dphi, left, right, 2 + h)
            dv = jnp.where(sides(h), matmul(phi_k[:, :SROWS], state), dv)
        grad += matmul_nt(acc[1, rows, :].astype(BF16), shift[...])
        dv = jnp.where(tail, dv, 0.0) + acc[2, rows, :]
        out_ref[rows, 0:128] = jnp.where(lane < 4 * FEAT, grad, 0.0).astype(BF16)
        out_ref[rows, 128:256] = dv.astype(BF16)
        return carry

    lax.fori_loop(0, 4, finish, 0)
    for cp in cps:
        cp.wait_send()


def taylor_backward(qkv, do, kept, seg, tables, jobs, count, collective):
    return step(
        functools.partial(taylor_backward_kernel, count),
        vmem(qkv, do, *kept, seg["col"], seg["row"], seg["last"], seg["before"], *tables)
        + [(seg["mix_back"], SMEM)],
        vmem(jax.ShapeDtypeStruct((1024, 256), BF16)),
        [
            VM((count, 4, SROWS, 128), BF16),
            VM((count, 4, 8, 256), F32),
            VM((3, 1024, 128), F32),
            VM((1024, 128), BF16),
            VM((2, 1024, 128), F32),
            pltpu.SemaphoreType.DMA((2, count)),
            pltpu.SemaphoreType.DMA((2, count)),
        ],
        jobs, 0, True, "taylor_backward", collective, 28,
    )


def rim_target(s, forward):
    hh, sh = lax.axis_index("hh"), lax.axis_index("sh")
    nhh, nsh = lax.axis_size("hh"), lax.axis_size("sh")
    if forward:
        wraps = jnp.where(hh == nhh - 1, 1, 0)
        slot = lax.rem(s + wraps, 4)
        leaves = wraps if s == 3 else 0
        return {"sh": lax.rem(sh + leaves, nsh), "hh": lax.rem(hh + 1, nhh)}, slot
    wraps = jnp.where(hh == 0, 1, 0)
    slot = lax.rem(s + 4 - wraps, 4)
    leaves = wraps if s == 0 else 0
    return {"sh": lax.rem(sh + nsh - leaves, nsh), "hh": lax.rem(hh + nhh - 1, nhh)}, slot


def window_mask(seg_col, seg_ext, rows, s):
    i = lax.broadcasted_iota(jnp.int32, (256, 256 + RIM), 0)
    j = lanes(256, 256 + RIM)
    return (j > i) & (j <= i + WINDOW) & (seg_col[rows, :] == seg_ext[s])


def window_probs(q, k, allowed):
    scores = jnp.where(allowed, matmul_nt(q, k) * 64**-0.5, -1e30)
    peak = jnp.max(scores, axis=1, keepdims=True)
    weights = jnp.exp(scores - peak)
    return weights / jnp.sum(weights, axis=1, keepdims=True)


def window_forward_kernel(begin, qkv, seg_col, seg_ext, o_ref, ext, rim, ssem, rsem):
    cps = []
    for s in range(4):
        target, slot = rim_target(s, True)
        src = qkv.at[pl.ds(s * 256 + 256 - RIM, RIM), pl.ds(128, 256)]
        cps.append(remote(src, rim.at[slot], ssem.at[s], rsem.at[slot], target))

    begin()

    def fill(s, carry):
        ext[s, RIM:, :] = qkv[pl.ds(s * 256, 256), 128:384]
        return carry

    lax.fori_loop(0, 4, fill, 0)
    for s in range(4):
        pltpu.make_async_copy(rim.at[s], rim.at[s], rsem.at[s]).wait()

    def run(s, carry):
        rows = pl.ds(s * 256, 256)
        ext[s, :RIM, :] = rim[s]
        q = qkv[rows, 0:128]
        k = ext[s, :, 0:128]
        v = ext[s, :, 128:256]
        left_half = lanes(256, 128) < 64
        allowed = window_mask(seg_col, seg_ext, rows, s)
        out = jnp.zeros((256, 128), F32)
        for h in range(2):
            side = left_half if h == 0 else jnp.logical_not(left_half)
            probs = window_probs(jnp.where(side, q, jnp.zeros((), BF16)), k, allowed)
            out = jnp.where(side, matmul(probs.astype(BF16), v), out)
        o_ref[rows, :] = out.astype(BF16)
        return carry

    lax.fori_loop(0, 4, run, 0)
    for cp in cps:
        cp.wait_send()


def window_forward(qkv, seg, jobs, collective):
    return step(
        window_forward_kernel,
        vmem(qkv, seg["col"], seg["ext"]),
        vmem(
            jax.ShapeDtypeStruct((1024, 128), BF16),
            jax.ShapeDtypeStruct((4, 256 + RIM, 256), BF16),
        ),
        [
            VM((4, RIM, 256), BF16),
            pltpu.SemaphoreType.DMA((4,)),
            pltpu.SemaphoreType.DMA((4,)),
        ],
        jobs, 0, True, "window_forward", collective, 14,
    )


def window_backward_kernel(
    begin, qkv, ext, do_ref, seg_col, seg_ext, part, u_ref, out_ref, mixed, acc, back, rim,
    ssem, rsem, own, cb, sb, keep, r1, r2, ss, rs,
):
    stages = scatter_rows(part, own, cb, sb, keep, r1, r2, ss, rs)
    next(stages)
    begin()
    zero = jnp.zeros((), BF16)

    def run(s, carry):
        rows = pl.ds(s * 256, 256)
        q = qkv[rows, 0:128]
        k = ext[s, :, 0:128]
        v = ext[s, :, 128:256]
        do = do_ref[rows, :]
        left_half = lanes(256, 128) < 64
        left_ext = lanes(256 + RIM, 128) < 64
        allowed = window_mask(seg_col, seg_ext, rows, s)
        dq = jnp.zeros((256, 128), F32)
        dk = jnp.zeros((256 + RIM, 128), F32)
        dv = jnp.zeros((256 + RIM, 128), F32)
        for h in range(2):
            side = left_half if h == 0 else jnp.logical_not(left_half)
            q_h = jnp.where(side, q, zero)
            do_h = jnp.where(side, do, zero)
            probs = window_probs(q_h, k, allowed)
            dprobs = matmul_nt(do_h, v)
            inner = jnp.sum(probs * dprobs, axis=1, keepdims=True)
            ds = (probs * (dprobs - inner)).astype(BF16)
            dq = jnp.where(side, matmul(ds, k), dq)
            dk += matmul_tn(ds, q_h)
            dv += matmul_tn(probs.astype(BF16), do_h)
        scale = 64**-0.5
        dk = dk * scale
        out_ref[rows, 0:128] = (dq * scale).astype(BF16)
        acc[rows, 0:128] = dk[RIM:]
        acc[rows, 128:256] = dv[RIM:]
        back[s, :, 0:128] = dk[:RIM].astype(BF16)
        back[s, :, 128:256] = dv[:RIM].astype(BF16)
        return carry

    lax.fori_loop(0, 4, run, 0)
    next(stages)
    cps = []
    for s in range(4):
        target, slot = rim_target(s, False)
        cps.append(remote(back.at[s], rim.at[slot], ssem.at[s], rsem.at[slot], target))
    next(stages)
    for s in range(4):
        pltpu.make_async_copy(rim.at[s], rim.at[s], rsem.at[s]).wait()

    def finish(s, carry):
        out_ref[pl.ds(s * 256, 256 - RIM), 128:384] = acc[pl.ds(s * 256, 256 - RIM), :].astype(BF16)
        rows = pl.ds(s * 256 + 256 - RIM, RIM)
        out_ref[rows, 128:384] = (acc[rows, :] + rim[s].astype(F32)).astype(BF16)
        return carry

    lax.fori_loop(0, 4, finish, 0)
    drain(stages)
    for half in range(2):
        mixed[half] = (u_ref[half] + own[half]).astype(BF16)
    for cp in cps:
        cp.wait_send()


def window_backward(qkv, ext, do, seg, part, u, jobs, collective):
    return step(
        window_backward_kernel,
        vmem(qkv, ext, do, seg["col"], seg["ext"], blocks(part), u),
        vmem(
            jax.ShapeDtypeStruct((1024, 384), BF16), jax.ShapeDtypeStruct((2, 64, D), BF16)
        ),
        [
            VM((1024, 256), F32),
            VM((4, RIM, 256), BF16),
            VM((4, RIM, 256), BF16),
            pltpu.SemaphoreType.DMA((4,)),
            pltpu.SemaphoreType.DMA((4,)),
        ]
        + rs_scratch(),
        jobs, 3, True, "window_backward", collective, 22,
    )


def row_routes():
    nsh, nhh = lax.axis_size("sh"), lax.axis_size("hh")
    groups = nsh * nhh
    routes = []
    for d in range(8 * groups):
        place, group = d // groups, d % groups
        s, c = place // 2, place % 2
        sh, hh = group // nhh, group % nhh
        routes.append((d, ((sh * 4 + s) * nhh + hh) * 2 + c))
    return routes


def segment_ids(lengths, positions):
    starts = jnp.cumsum(lengths) - lengths
    return jnp.sum((positions[..., None] >= starts).astype(jnp.int32), axis=-1) - 1


def segments(lengths, stretch):
    nsh, nhh = lax.axis_size("sh"), lax.axis_size("hh")
    sh, hh = lax.axis_index("sh"), lax.axis_index("hh")
    mine = (sh * 4 + jnp.arange(4, dtype=jnp.int32)) * nhh + hh
    first = mine * 256
    tokens = segment_ids(lengths, first[:, None] + jnp.arange(256, dtype=jnp.int32))
    ext = segment_ids(lengths, first[:, None] - RIM + jnp.arange(256 + RIM, dtype=jnp.int32))
    before = segment_ids(lengths, first - 1)
    last = tokens[:, -1]
    gsh, ghh, gs = jnp.meshgrid(
        jnp.arange(nsh), jnp.arange(nhh), jnp.arange(4), indexing="ij"
    )
    others = ((gsh * 4 + gs) * nhh + ghh).reshape(-1).astype(jnp.int32)
    others_last = segment_ids(lengths, others * 256 + 255)
    others_before = segment_ids(lengths, others * 256 - 1)
    mix = (others[None] < mine[:, None]) & (others_last[None] == before[:, None])
    mix_back = (others[None] > mine[:, None]) & (others_before[None] == last[:, None])
    wide = lambda a: jnp.broadcast_to(a[:, None], (4, 256)).reshape(1024, 1)
    return {
        "col": tokens.reshape(1024, 1),
        "row": tokens.reshape(4, 1, 256),
        "ext": ext.reshape(4, 1, 256 + RIM),
        "last": wide(last),
        "before": wide(before),
        "mix": mix.astype(F32),
        "mix_back": mix_back.astype(F32),
    }


def spread_ff(member):
    rows = member.shape[0]
    width = -(-member.shape[1] // (NTP * 128)) * 128
    padded = jnp.pad(member, ((0, 0), (0, NTP * width - member.shape[1])))
    return padded.reshape(rows, NTP, width)


def on_device(
    layer_input, lengths, gain_a1, lin_q, lin_k, lin_v, lin_out, gain_a2, mlp_a_gate, mlp_a_up,
    mlp_a_down, gain_b1, win_q, win_k, win_v, win_out, gain_b2, mlp_b_gate, mlp_b_up, mlp_b_down,
    cotangent,
):
    count = lax.axis_size(GROUP)
    rows = lin_q.shape[0]
    hidden_size = mlp_a_gate.shape[1]
    gains = jnp.pad(jnp.stack([gain_a1, gain_a2, gain_b1, gain_b2], axis=1), ((0, 0), (0, 60)))
    gains = jnp.broadcast_to(gains[:, None, :], (rows, NTP, 64))
    seg = segments(lengths, 0)
    tables = taylor_tables()

    split = lambda member: member.reshape(rows, NTP, -1)
    bundle_lin = jnp.concatenate(
        [split(lin_q), split(lin_k), gains, split(lin_v)], axis=-1
    ).transpose(1, 0, 2)
    bundle_a = jnp.concatenate(
        [spread_ff(mlp_a_gate), spread_ff(mlp_a_up), spread_ff(mlp_a_down.T)], axis=-1
    ).transpose(1, 0, 2)
    bundle_win = jnp.concatenate([split(win_q), split(win_k), split(win_v)], axis=-1).transpose(
        1, 0, 2
    )
    bundle_b = jnp.concatenate(
        [spread_ff(mlp_b_gate), spread_ff(mlp_b_up), spread_ff(mlp_b_down.T)], axis=-1
    ).transpose(1, 0, 2)
    ff = bundle_a.shape[-1] // 3
    width = bundle_lin.shape[-1]
    nsh, nhh = lax.axis_size("sh"), lax.axis_size("hh")
    places = lambda a: a.reshape(4, 2, rows, a.shape[-1])
    whole = lambda a: a.reshape(D, a.shape[-1])
    parts = lambda a: a.astype(BF16).reshape(nsh * 4, nhh, 2, rows, a.shape[-1])
    total = lambda a: jnp.sum(a.astype(F32), axis=0).astype(BF16)
    own_lin_out = lax.ppermute(lin_out, AXES, row_routes())
    own_win_out = lax.ppermute(win_out, AXES, row_routes())

    x_own = layer_input.reshape(2, 64, D)
    cot_own = cotangent.reshape(2, 64, D)
    (x_full, _, w_lin), (mid_a, mid_win, mid_b) = first(
        x_own, places(bundle_lin),
        [Job("pa", places(bundle_a)), Job("pa", places(bundle_win)), Job("pa", places(bundle_b))], 1,
    )
    w_lin = whole(w_lin)
    gains = w_lin[:, 64:68].astype(F32).T
    g_a1, g_a2, g_b1, g_b2 = (gains[i : i + 1] for i in range(4))
    w_lin = jnp.concatenate([w_lin[:, :64], jnp.zeros((D, 64), BF16), w_lin[:, 128:]], axis=1)
    n_a1 = normed_half(flat(x_full).astype(F32), g_a1)
    qkv_a = matmul(n_a1, w_lin).astype(BF16)
    (o_a, *kept, cot), (w_gate_a, w_lin_out) = taylor_forward(
        qkv_a, seg, tables, cot_own, [Job("zg", mid_a, (0, ff)), Job("zr", own_lin_out)], count, 2
    )
    cot, w_lin_out = flat(cot), w_lin_out.reshape(128, D)
    part = matmul(o_a, w_lin_out).astype(BF16)
    (h_a, n_a2), (w_up_a, w_down_a) = forward_step(
        part, x_own.astype(F32), g_a2, [Job("zg", mid_a, (ff, ff)), Job("zg", mid_a, (2 * ff, ff))], 3
    )
    n_a2 = flat(n_a2)
    w_a = (whole(w_gate_a), whole(w_up_a), whole(w_down_a))

    def mlp_forward(n, w):
        gate, up = matmul(n, w[0]), matmul(n, w[1])
        hidden = (gate / (1.0 + jnp.exp(-gate)) * up).astype(BF16)
        return gate, up, hidden, matmul_nt(hidden, w[2]).astype(BF16)

    def mlp_backward(n, w, gate, up, hidden, upstream):
        dhidden = matmul(upstream, w[2])
        sig = 1.0 / (1.0 + jnp.exp(-gate))
        dgate = (dhidden * up * sig * (1.0 + gate * (1.0 - sig))).astype(BF16)
        dup = (dhidden * gate * sig).astype(BF16)
        part = (matmul_nt(dgate, w[0]) + matmul_nt(dup, w[1])).astype(BF16)
        both = jnp.concatenate([dgate, dup], axis=1)
        return part, parts(matmul_tn(n, both)), parts(matmul_tn(upstream, hidden))

    gate_a, up_a, hidden_a, part = mlp_forward(n_a2, w_a)
    (out_a, n_b1), (w_win, w_gate_b) = forward_step(
        part, h_a, g_b1, [Job("zg", mid_win), Job("zg", mid_b, (0, ff))], 4
    )
    n_b1, w_win = flat(n_b1), whole(w_win)
    qkv_b = matmul(n_b1, w_win).astype(BF16)
    (o_b, ext), (w_win_out,) = window_forward(qkv_b, seg, [Job("zr", own_win_out)], 5)
    w_win_out = w_win_out.reshape(128, D)
    part = matmul(o_b, w_win_out).astype(BF16)
    (h_b, n_b2), (w_up_b, w_down_b) = forward_step(
        part, out_a, g_b2, [Job("zg", mid_b, (ff, ff)), Job("zg", mid_b, (2 * ff, ff))], 6
    )
    n_b2 = flat(n_b2)
    w_b = (whole(w_gate_b), whole(w_up_b), whole(w_down_b))
    gate_b, up_b, hidden_b, part_out = mlp_forward(n_b2, w_b)

    part, grad_gu_b, grad_down_b = mlp_backward(n_b2, w_b, gate_b, up_b, hidden_b, cot)
    (grad_h_b, gg_b2, up_full), (gu_b,) = backward_step(
        part, h_b, g_b2, cot_own, [Job("zs", grad_gu_b)], 7
    )
    up_full = flat(up_full)
    do_b = matmul_nt(up_full, w_win_out).astype(BF16)
    grad_win_out = matmul_tn(o_b, up_full).astype(BF16).reshape(count, -1, D)
    (dqkv_b, mixed), (down_b,) = window_backward(
        qkv_b, ext, do_b, seg, part_out, h_b, [Job("zs", grad_down_b)], 8
    )
    part = matmul_nt(dqkv_b, w_win).astype(BF16)
    grad_win = parts(matmul_tn(n_b1, dqkv_b))
    (grad_out_a, gg_b1, up_full), (win, win_out_t, gu_b) = backward_step(
        part, out_a, g_b1, grad_h_b,
        [Job("zs", grad_win), Job("zt", grad_win_out), Job("pa", total(gu_b))], 9,
    )
    up_full = flat(up_full)
    part, grad_gu_a, grad_down_a = mlp_backward(n_a2, w_a, gate_a, up_a, hidden_a, up_full)
    (grad_h_a, gg_a2, up_full), (gu_a, down_b) = backward_step(
        part, h_a, g_a2, grad_out_a, [Job("zs", grad_gu_a), Job("pa", total(down_b))], 10
    )
    up_full = flat(up_full)
    do_a = matmul_nt(up_full, w_lin_out).astype(BF16)
    grad_lin_out = matmul_tn(o_a, up_full).astype(BF16).reshape(count, -1, D)
    (dqkv_a,), (down_a, win, gu_a) = taylor_backward(
        qkv_a, do_a, kept, seg, tables,
        [Job("zs", grad_down_a), Job("pa", total(win)), Job("pa", total(gu_a))], count, 11,
    )
    part = matmul_nt(dqkv_a, w_lin).astype(BF16)
    rows_a = flat(x_full).astype(F32)
    rows_a = rows_a * lax.rsqrt(jnp.mean(rows_a * rows_a, axis=-1, keepdims=True) + EPSILON)
    gg_a1 = jnp.sum(part.astype(F32) * rows_a, axis=0, keepdims=True)
    gg = jnp.concatenate([gg_a1, gg_a2, gg_b1, gg_b2, jnp.zeros((60, D), F32)], axis=0).T
    grad_lin = matmul_tn(n_a1, dqkv_a)
    grad_lin = parts(jnp.concatenate([grad_lin[:, :64], gg, grad_lin[:, 128:]], axis=1))
    (grad_input, _), (lin, lin_out_t, down_a) = backward_step(
        part, x_own, g_a1, grad_h_a,
        [Job("zs", grad_lin), Job("zt", grad_lin_out), Job("pa", total(down_a))], 12, last=True,
    )
    _, (lin_g,) = step(
        lambda begin: None, [], [], [], [Job("pa", total(lin))], 7, False, "last", 13, 5
    )

    def joined(a, lo, hi):
        a = a.reshape(NTP, rows, -1)[:, :, lo:hi].astype(F32)
        return a.transpose(1, 0, 2).reshape(rows, -1)

    def unpack_mlp(gate_up, down):
        return (
            joined(gate_up, 0, ff)[:, :hidden_size],
            joined(gate_up, ff, 2 * ff)[:, :hidden_size],
            joined(down, 0, ff)[:, :hidden_size].T,
        )

    gate_b_g, up_b_g, down_b_g = unpack_mlp(gu_b, down_b)
    gate_a_g, up_a_g, down_a_g = unpack_mlp(gu_a, down_a)
    back = [(b, a) for a, b in row_routes()]
    win_out_g = lax.ppermute(total(win_out_t), AXES, back).astype(F32)
    lin_out_g = lax.ppermute(total(lin_out_t), AXES, back).astype(F32)
    gg = jnp.sum(lin_g.reshape(NTP, rows, width)[:, :, 64:68].astype(F32), axis=0)
    return (
        mixed.reshape(128, D),
        grad_input.reshape(128, D),
        gg[:, 0],
        joined(lin_g, 0, 32),
        joined(lin_g, 32, 64),
        joined(lin_g, 128, 256),
        lin_out_g,
        gg[:, 1],
        gate_a_g,
        up_a_g,
        down_a_g,
        gg[:, 2],
        joined(win, 0, 128),
        joined(win, 128, 256),
        joined(win, 256, 384),
        win_out_g,
        gg[:, 3],
        gate_b_g,
        up_b_g,
        down_b_g,
    )


def solution(mesh):
    seq, head = mesh.devices.shape
    fine = Mesh(mesh.devices.reshape(seq // 4, 2, 2, head // 2, 2), AXES)
    row, vec, col = P(AXES, None), P(AXES), P(None, AXES)
    placed = (
        row, P(), vec, row, row, row, row, vec, row, row, col,
        vec, row, row, row, row, vec, row, row, col, row,
    )
    out = (
        row, row, vec, row, row, row, row, vec, row, row, col,
        vec, row, row, row, row, vec, row, row, col,
    )
    return jax.shard_map(on_device, mesh=fine, in_specs=placed, out_specs=out, check_vma=False)
```

time: 3150 us -> 581 us (0.18)
  waiting for transfers between devices: 2490 us -> 0.01 us
  Pallas kernels: 0 us -> 441 us
  blocking collectives: 246 us -> 0 us
  matrix products: 234 us -> 68 us
  local copies, waits for them, and re-layouts: 80.1 us -> 24.8 us
    reduce_scatter x14 -> x0, waiting for transfers between devices: 1970 us -> none  [the longest x2 323 us: summed_layer(): lax.psum_scatter(grad_down, ('seq', 'head'), scatter_dimension=1, tiled=T...]
    pallas_call x0 -> x13, Pallas kernels: none -> 441 us  [step(): pl.pallas_call(kernel, out_shape=tuple((o for o, _ in outs)) + tuple((job...]
    all_gather x12 -> x0, waiting for transfers between devices: 438 us -> none  [the longest x1 64.2 us: on_device(): lax.all_gather(mlp_b_up, ('seq', 'head'), axis=0, tiled=True)]
    dot_general x55 -> x10, matrix products: 147 us -> 23.6 us  [matmul(): return jnp.dot(left, right, preferred_element_type=F32)]
    all_gather x6 -> x0, blocking collectives: 119 us -> none  [the longest x1 42.9 us: on_device(): lax.all_gather(lin_q, ('seq', 'head'), axis=0, tiled=True)]
    unnamed x3 -> x0, blocking collectives: 88.7 us -> none
    all_to_all x6 -> x0, waiting for transfers between devices: 69.3 us -> none  [the longest x1 21.5 us: on_device(): lax.all_to_all(split_groups((window_q, window_k, window_v), groups), 'hea...]
    all_to_all x2 -> x0, blocking collectives: 38.5 us -> none  [the longest x1 23.4 us: on_device(): lax.all_to_all(packed_gb[:, None, :], 'head', split_axis=0, concat_axis=1...]
  transfers between devices with their start and end apart: 34 -> 4, of which waited for: 29 -> 0; matrix products, arithmetic and copies ran while one was open for 6% -> 9% of each run, Pallas kernels for 0% -> 30%
where the time goes in v1:
time: 581 us; the launch traced here: 571 us
  Pallas kernels  441 us (76%)
  matrix products  68 us (12%)
  other arithmetic  31.1 us (5%)
  local copies, waits for them, and re-layouts  24.8 us (4%)
    pallas_call x13, Pallas kernels, step(): pl.pallas_call(kernel, out_shape=tuple((o for o, _ in outs)) + tuple((job...  441 us
    dot_general x10, matrix products, matmul(): return jnp.dot(left, right, preferred_element_type=F32)  23.6 us
    dot_general x8, matrix products, matmul_tn(): lax.dot_general(left, right, (((0,), (0,)), ((), ())), preferred_element_...  23.4 us
    dot_general x10, matrix products, matmul_nt(): lax.dot_general(left, right, (((1,), (1,)), ((), ())), preferred_element_...  21 us
  transfers between devices with their start and end apart: 4, of which 0 were waited for; matrix products, arithmetic and copies ran while one was open for 9% of the time, Pallas kernels for 30%

profile of v1, /device:TPU:0, one launch (start us, length us, event | category | flops | bytes accessed | tf_op | source)
XLA Modules:
  0.0 570.9 jit_solution(2824436927789527932)
XLA Ops:
  14.5 41.8 %first.1 = (bf16[4,2,2,64,1024]{4,3,2,1,0:T(8,128)(2,1)}, bf16[4,2,32,256]{3,2,1,0:T(8,128)(2,1)}, bf16[4,4,2,32,256]{4,3,2,1,0:T(8,128)(2,1)}, bf16[4,2,32,1152...) custom-call(bf16[2,64,1024]{2,1,0:T(8,128)(2,1)} %bitcast.255, ...), custom_call_target="tpu_custom_call" | custom-call | bytes 75000000 | tf_op jit(solution)/shard_map/first/pallas_call | solution.py:317
  72.6 49.8 %taylor_forward.1 = (bf16[1024,128]{1,0:T(8,128)(2,1)}, f32[1024,128]{1,0:T(8,128)}, f32[1024,128]{1,0:T(8,128)}, bf16[4,160,128]{2,1,0:T(8,128)(2,1)}, f32[4,8,...) custom-call(bf16[1024,256]{1,0:T(8,128)(2,1)} %convolution_convert_f, ...), custom_call_target="tpu_custom_call" | custom-call | bytes 84000000 | tf_op jit(solution)/shard_map/taylor_forward/pallas_call | solution.py:317
  122.4 3.1 convolution_convert_fusion.5
  125.5 37.6 %forward_step.3 = (f32[2,64,1024]{2,1,0:T(8,128)}, bf16[4,2,2,64,1024]{4,3,2,1,0:T(8,128)(2,1)}, bf16[4,4,2,32,384]{4,3,2,1,0:T(8,128)(2,1)}, bf16[4,4,2,32,384]{4,3,2,1,0:T(8,128)(2,1)}) custom-call(bf16[4,2,2,64,1024]{4,3,2,1,0:T(8,128)(2,1)} %bitcast.247, f32[2,64,1024]{2,1,0:T(8,128)} %convert_element_type.180.refs_1_, ...), custom_call_target="tpu_custom_call" | custom-call | bytes 84000000 | tf_op jit(solution)/shard_map/forward_step/pallas_call | solution.py:317
  163.1 2.8 fusion.16
  165.9 2.3 multiply_convert_fusion.6
  168.2 2.7 convolution_convert_fusion.2
  170.9 40.8 %forward_step.4 = (f32[2,64,1024]{2,1,0:T(8,128)}, bf16[4,2,2,64,1024]{4,3,2,1,0:T(8,128)(2,1)}, bf16[4,4,2,32,384]{4,3,2,1,0:T(8,128)(2,1)}, bf16[4,4,2,32,384]{4,3,2,1,0:T(8,128)(2,1)}) custom-call(bf16[4,2,2,64,1024]{4,3,2,1,0:T(8,128)(2,1)} %bitcast.262, f32[2,64,1024]{2,1,0:T(8,128)} %get-tuple-element.83.refs_1_, ...), custom_call_target="tpu_custom_call" | custom-call | bytes 84000000 | tf_op jit(solution)/shard_map/forward_step/pallas_call | solution.py:317
  211.7 3.9 convolution_convert_fusion.11.refs_0_
  216.3 15.7 %window_forward.1 = (bf16[1024,128]{1,0:T(8,128)(2,1)}, bf16[4,320,256]{2,1,0:T(8,128)(2,1)}, bf16[4,32,1024]{2,1,0:T(8,128)(2,1)}) custom-call(bf16[1024,384]{1,0:T(8,128)(2,1)} %convolution_convert_fusion.11.refs_0_, s32[1024,1]{1,0:T(8,128)} %bitcast.240, s32[4,1,320]{2,1,0:T(1,128)} %sub.54.refs_2_.refs_4_, bf16[32,1024]{1,0:T(8,128)(2,1)} %copy-done.34), custom_call_target="tpu_custom_call" | custom-call | bytes 42000000 | tf_op jit(solution)/shard_map/window_forward/pallas_call | solution.py:317
  232.0 3.1 convolution_convert_fusion.4
  235.1 36.7 %forward_step.5 = (f32[2,64,1024]{2,1,0:T(8,128)}, bf16[4,2,2,64,1024]{4,3,2,1,0:T(8,128)(2,1)}, bf16[4,4,2,32,384]{4,3,2,1,0:T(8,128)(2,1)}, bf16[4,4,2,32,384]{4,3,2,1,0:T(8,128)(2,1)}) custom-call(bf16[4,2,2,64,1024]{4,3,2,1,0:T(8,128)(2,1)} %bitcast.248, f32[2,64,1024]{2,1,0:T(8,128)} %get-tuple-element.92.refs_1_, ...), custom_call_target="tpu_custom_call" | custom-call | bytes 84000000 | tf_op jit(solution)/shard_map/forward_step/pallas_call | solution.py:317
  271.8 2.8 fusion.18
  280.2 2.7 convolution_convert_fusion.1
  284.2 3.0 convolution_convert_fusion.7
  287.3 2.7 add_convert_fusion.1
  289.9 37.3 %backward_step.3 = (f32[2,64,1024]{2,1,0:T(8,128)}, f32[1,1024]{1,0:T(1,128)}, bf16[4,2,2,64,1024]{4,3,2,1,0:T(8,128)(2,1)}, bf16[4,4,2,32,768]{4,3,2,1,0:T(8,128)(2,1)}) custom-call(bf16[4,2,2,64,1024]{4,3,2,1,0:T(8,128)(2,1)} %bitcast.249, f32[2,64,1024]{2,1,0:T(8,128)} %get-tuple-element.97.refs_1_.refs_6_, f32[1,1024]{1,0:T(1,128)} %get-tuple-element.148.refs_2_, ...), custom_call_target="tpu_custom_call" | custom-call | bytes 84000000 | tf_op jit(solution)/shard_map/backward_step/pallas_call | solution.py:317
  327.3 2.9 convolution_convert_fusion.16
  331.7 29.8 %window_backward.1 = (bf16[1024,384]{1,0:T(8,128)(2,1)}, bf16[2,64,1024]{2,1,0:T(8,128)(2,1)}, bf16[4,4,2,32,384]{4,3,2,1,0:T(8,128)(2,1)}) custom-call(bf16[1024,384]{1,0:T(8,128)(2,1)} %convolution_convert_fusion.11.refs_0_, bf16[4,320,256]{2,1,0:T(8,128)(2,1)} %get-tuple-element.88.refs_1_, bf16[1024,128]{1,0:T(8,128)(2,1)} %convolution_convert_fusion.17.refs_2_, ...), custom_call_target="tpu_custom_call" | custom-call | bytes 66000000 | tf_op jit(solution)/shard_map/window_backward/pallas_call | solution.py:317
  361.5 3.4 convolution_convert_fusion.9
  364.9 2.7 convolution_convert_fusion
  369.6 2.5 reduce_sum.177.refs_6_
  372.1 35.1 %backward_step.4 = (f32[2,64,1024]{2,1,0:T(8,128)}, f32[1,1024]{1,0:T(1,128)}, bf16[4,2,2,64,1024]{4,3,2,1,0:T(8,128)(2,1)}, bf16[4,4,2,32,384]{4,3,2,1,0:T(8,12...) custom-call(bf16[4,2,2,64,1024]{4,3,2,1,0:T(8,128)(2,1)} %bitcast.263, ...), custom_call_target="tpu_custom_call" | custom-call | bytes 84000000 | tf_op jit(solution)/shard_map/backward_step/pallas_call | solution.py:317
  407.3 3.9 convolution_convert_fusion.8
  414.3 3.1 convolution_convert_fusion.6
  417.4 2.7 add_convert_fusion
  420.1 35.4 %backward_step.5 = (f32[2,64,1024]{2,1,0:T(8,128)}, f32[1,1024]{1,0:T(1,128)}, bf16[4,2,2,64,1024]{4,3,2,1,0:T(8,128)(2,1)}, bf16[4,4,2,32,768]{4,3,2,1,0:T(8,128)(2,1)}, bf16[4,2,32,384]{3,2,1,0:T(8,128)(2,1)}) custom-call(bf16[4,2,2,64,1024]{4,3,2,1,0:T(8,128)(2,1)} %bitcast.250, f32[2,64,1024]{2,1,0:T(8,128)} %get-tuple-element.83.refs_1_, ...), custom_call_target="tpu_custom_call" | custom-call | bytes 84000000 | tf_op jit(solution)/shard_map/backward_step/pallas_call | solution.py:317
  455.5 2.9 convolution_convert_fusion.14
  460.7 2.6 reduce_sum.181.refs_16_
  463.2 50.2 %taylor_backward.1 = (bf16[1024,256]{1,0:T(8,128)(2,1)}, bf16[4,4,2,32,384]{4,3,2,1,0:T(8,128)(2,1)}, bf16[4,2,32,384]{3,2,1,0:T(8,128)(2,1)}, bf16[4,2,32,768]{3,2,1,0:T(8,128)(2,1)}) custom-call(bf16[1024,256]{1,0:T(8,128)(2,1)} %convolution_convert_fusion.13.refs_0_, bf16[1024,128]{1,0:T(8,128)(2,1)} %convolution_convert_fusion.15.refs_1_, ...), custom_call_target="tpu_custom_call" | custom-call | bytes 84000000 | tf_op jit(solution)/shard_map/taylor_backward/pallas_call | solution.py:317
  521.5 24.6 %last_backward.1 = (f32[2,64,1024]{2,1,0:T(8,128)}, f32[1,1024]{1,0:T(1,128)}, bf16[4,4,2,32,256]{4,3,2,1,0:T(8,128)(2,1)}, bf16[4,32,1024]{2,1,0:T(8,128)(2,1)}, bf16[4,2,32,384]{3,2,1,0:T(8,128)(2,1)}) custom-call(bf16[4,2,2,64,1024]{4,3,2,1,0:T(8,128)(2,1)} %bitcast.261, bf16[2,64,1024]{2,1,0:T(8,128)(2,1)} %bitcast.256, f32[1,1024]{1,0:T(1,128)} %copy-done.35, ...), custom_call_target="tpu_custom_call" | custom-call | bytes 48000000 | tf_op jit(solution)/shard_map/last_backward/pallas_call | solution.py:317
  547.9 5.6 last.1
  (250 shorter events, 72.7 us)
Async XLA Ops:
  0.7 10.4 %copy-start = (bf16[32,1024]{1,0:T(8,128)(2,1)S(1)}, bf16[32,1024]{1,0:T(8,128)(2,1)}, u32[]{:S(2)}) copy-start(bf16[32,1024]{1,0:T(8,128)(2,1)} %param.37) | copy-start | bytes 196612
  0.7 10.3 %copy-start.29 = (bf16[32,2752]{1,0:T(8,128)(2,1)S(1)}, bf16[32,2752]{1,0:T(8,128)(2,1)}, u32[]{:S(2)}) copy-start(bf16[32,2752]{1,0:T(8,128)(2,1)} %param.41) | copy-start | bytes 528388
  0.7 10.3 %copy-start.30 = (bf16[32,2752]{1,0:T(8,128)(2,1)S(1)}, bf16[32,2752]{1,0:T(8,128)(2,1)}, u32[]{:S(2)}) copy-start(bf16[32,2752]{1,0:T(8,128)(2,1)} %param.42) | copy-start | bytes 528388
  0.7 10.4 %copy-start.31 = (bf16[2752,32]{0,1:T(8,128)(2,1)S(1)}, bf16[2752,32]{0,1:T(8,128)(2,1)}, u32[]{:S(2)}) copy-start(bf16[2752,32]{0,1:T(8,128)(2,1)} %param.43) | copy-start | bytes 528388
  0.7 10.4 %copy-start.33 = (bf16[32,1024]{1,0:T(8,128)(2,1)S(1)}, bf16[32,1024]{1,0:T(8,128)(2,1)}, u32[]{:S(2)}) copy-start(bf16[32,1024]{1,0:T(8,128)(2,1)} %param.38) | copy-start | bytes 196612
  0.7 71.2 %collective-permute-start = (bf16[32,1024]{1,0:T(8,128)(2,1)}, bf16[32,1024]{1,0:T(8,128)(2,1)S(1)}, u32[]{:S(2)}, u32[]{:S(2)}) collective-permute-start(bf16[32,1024]{1,0:T(8,128)(2,1)} %param.30), channel_id=1, source_target_pairs={{0,0},{1,2},{2,4},{3,6},{4,1},{5,3},{6,5},{7,7},{8,8},{9,10},{10,1... | collective-permute-start | bytes 196616 | tf_op jit(solution)/shard_map/ppermute | solution.py:1025
  2.3 213.3 %collective-permute-start.1 = (bf16[32,1024]{1,0:T(8,128)(2,1)}, bf16[32,1024]{1,0:T(8,128)(2,1)S(1)}, u32[]{:S(2)}, u32[]{:S(2)}) collective-permute-start(bf16[32,1024]{1,0:T(8,128)(2,1)} %param.39), channel_id=1, source_target_pairs={{0,0},{1,2},{2,4},{3,6},{4,1},{5,3},{6,5},{7,7},{8,8},{9,10},{10,1... | collective-permute-start | bytes 196616 | tf_op jit(solution)/shard_map/ppermute | solution.py:1026
  13.7 45.8 %copy-start.51 = (s32[5]{0:T(128)S(1)}, s32[5]{0:T(128)}, u32[]{:S(2)}) copy-start(s32[5]{0:T(128)} %param.25) | copy-start | bytes 64
  57.3 6.5 %copy-start.4 = (bf16[4,2,2,64,1024]{4,3,2,1,0:T(8,128)(2,1)S(1)}, bf16[4,2,2,64,1024]{4,3,2,1,0:T(8,128)(2,1)}, u32[]{:S(2)}) copy-start(bf16[4,2,2,64,1024]{4,3,2,1,0:T(8,128)(2,1)} %get-tuple-element.74) | copy-start | bytes 6291460
  125.5 37.6 %copy-start.17 = (bf16[4,4,2,32,384]{4,3,2,1,0:T(8,128)(2,1)S(1)}, bf16[4,4,2,32,384]{4,3,2,1,0:T(8,128)(2,1)}, u32[]{:S(2)}) copy-start(bf16[4,4,2,32,384]{4,3,2,1,0:T(8,128)(2,1)} %get-tuple-element.80) | copy-start | bytes 2359300
  168.2 43.5 %copy-start.52 = (bf16[1024,384]{0,1:T(8,128)(2,1)}, bf16[1024,384]{0,1:T(8,128)(2,1)S(1)}, u32[]{:S(2)}) copy-start(bf16[1024,384]{0,1:T(8,128)(2,1)S(1)} %get-tuple-element.158) | copy-start | bytes 2359300
  235.1 36.7 %copy-start.14 = (bf16[4,4,2,32,384]{4,3,2,1,0:T(8,128)(2,1)S(1)}, bf16[4,4,2,32,384]{4,3,2,1,0:T(8,128)(2,1)}, u32[]{:S(2)}) copy-start(bf16[4,4,2,32,384]{4,3,2,1,0:T(8,128)(2,1)} %get-tuple-element.96) | copy-start | bytes 2359300
  289.9 37.4 %copy-start.11 = (bf16[1024,128]{1,0:T(8,128)(2,1)S(1)}, bf16[1024,128]{1,0:T(8,128)(2,1)}, u32[]{:S(2)}) copy-start(bf16[1024,128]{1,0:T(8,128)(2,1)} %get-tuple-element.90) | copy-start | bytes 786436
  331.7 29.8 %copy-start.41 = (bf16[4,2,2,64,1024]{4,3,2,1,0:T(8,128)(2,1)S(1)}, bf16[4,2,2,64,1024]{4,3,2,1,0:T(8,128)(2,1)}, u32[]{:S(2)}) copy-start(bf16[4,2,2,64,1024]{4,3,2,1,0:T(8,128)(2,1)} %get-tuple-element.86) | copy-start | bytes 6291460
  372.1 35.2 %copy-start.53 = (bf16[1024,384]{0,1:T(8,128)(2,1)S(1)}, bf16[1024,384]{0,1:T(8,128)(2,1)}, u32[]{:S(2)}) copy-start(bf16[1024,384]{0,1:T(8,128)(2,1)} %copy-done.52) | copy-start | bytes 2359300
  407.2 4.0 copy-start.44
  407.3 4.0 copy-start.46
  407.3 4.0 copy-start.55
  420.1 35.4 %copy-start.9 = (bf16[1024,128]{1,0:T(8,128)(2,1)S(1)}, bf16[1024,128]{1,0:T(8,128)(2,1)}, u32[]{:S(2)}) copy-start(bf16[1024,128]{1,0:T(8,128)(2,1)} %get-tuple-element.77) | copy-start | bytes 786436
  455.5 4.4 copy-start.15
  463.2 50.2 %copy-start.7 = (bf16[1024,1024]{1,0:T(8,128)(2,1)S(1)}, bf16[1024,1024]{1,0:T(8,128)(2,1)}, u32[]{:S(2)}) copy-start(bf16[1024,1024]{1,0:T(8,128)(2,1)} %copy-done.6) | copy-start | bytes 6291460
  521.5 35.6 %copy-start.23 = (bf16[4,32,1024]{2,1,0:T(8,128)(2,1)S(1)}, bf16[4,32,1024]{2,1,0:T(8,128)(2,1)}, u32[]{:S(2)}) copy-start(bf16[4,32,1024]{2,1,0:T(8,128)(2,1)} %get-tuple-element.125) | copy-start | bytes 786436
  521.5 36.3 %copy-start.21 = (bf16[4,2,32,768]{3,2,1,0:T(8,128)(2,1)S(1)}, bf16[4,2,32,768]{3,2,1,0:T(8,128)(2,1)}, u32[]{:S(2)}) copy-start(bf16[4,2,32,768]{3,2,1,0:T(8,128)(2,1)} %get-tuple-element.126) | copy-start | bytes 1179652
  547.9 11.5 %copy-start.26 = (bf16[4,2,32,384]{3,2,1,0:T(8,128)(2,1)S(1)}, bf16[4,2,32,384]{3,2,1,0:T(8,128)(2,1)}, u32[]{:S(2)}) copy-start(bf16[4,2,32,384]{3,2,1,0:T(8,128)(2,1)} %get-tuple-element.127) | copy-start | bytes 589828
  556.0 4.2 copy-start.22
  557.1 10.8 %collective-permute-start.3 = (bf16[32,1024]{1,0:T(8,128)(2,1)S(1)}, bf16[32,1024]{1,0:T(8,128)(2,1)S(1)}, u32[]{:S(2)}, u32[]{:S(2)}) collective-permute-start(bf16[32,1024]{1,0:T(8,128)(2,1)S(1)} %reduce_sum.187), channel_id=1, source_target_pairs={{0,0},{2,1},{4,2},{6,3},{1,4},{3,5},{5,6},{7,7},{8,8},{10,9},{12,1... | collective-permute-start | bytes 196616 | tf_op jit(solution)/shard_map/ppermute | solution.py:1138
  559.4 4.9 copy-start.27
  560.2 4.8 copy-start.28
  561.8 7.4 %copy-start.25 = (bf16[2,64,1024]{2,1,0:T(8,128)(2,1)S(1)}, bf16[2,64,1024]{2,1,0:T(8,128)(2,1)}, u32[]{:S(2)}) copy-start(bf16[2,64,1024]{2,1,0:T(8,128)(2,1)} %get-tuple-element.99) | copy-start | bytes 786436
  561.9 8.0 %copy-start.20 = (f32[2,64,1024]{2,1,0:T(8,128)S(1)}, f32[2,64,1024]{2,1,0:T(8,128)}, u32[]{:S(2)}) copy-start(f32[2,64,1024]{2,1,0:T(8,128)} %get-tuple-element.119) | copy-start | bytes 1572868
  561.9 6.6 %collective-permute-start.2 = (bf16[32,1024]{1,0:T(8,128)(2,1)S(1)}, bf16[32,1024]{1,0:T(8,128)(2,1)S(1)}, u32[]{:S(2)}, u32[]{:S(2)}) collective-permute-start(bf16[32,1024]{1,0:T(8,128)(2,1)S(1)} %reduce_sum.186), channel_id=1, source_target_pairs={{0,0},{2,1},{4,2},{6,3},{1,4},{3,5},{5,6},{7,7},{8,8},{10,9},{12,1... | collective-permute-start | bytes 196616 | tf_op jit(solution)/shard_map/ppermute | solution.py:1139
  564.3 6.4 %copy-start.1 = (bf16[32,1024]{1,0:T(8,128)(2,1)S(1)}, bf16[32,1024]{1,0:T(8,128)(2,1)}, u32[]{:S(2)}) copy-start(bf16[32,1024]{1,0:T(8,128)(2,1)} %param.37) | copy-start | bytes 196612
  (31 other events, 74.5 us)
